TPU v7x, 256 devices: a whole 4x4x8 slice. The times are simulated.
256 devices in a mesh: cohort: 64 (over x, z, y_hi), variant: 4 (over y_lo, core).
Axes of the slice: x: 4, y: 4 (y_hi: 2, y_lo: 2; y = y_hi * 2 + y_lo), z: 8, core: 2. Of those that a mesh axis runs over, the one named last changes fastest.
Arguments:
- probs: bfloat16 [3, 32768, 3072], P(None, 'cohort', 'variant'), may hold values from 0 to 1, as said below
- cohort_sizes: int32 [42], replicated, may hold values from 1 to 1024, 32768 in all
Outputs:
- kinship: float32 [32768, 2560], P('cohort', 'variant')
Inputs may be any that keep to these rules, and one draw needn't show every extreme that they name: `cohort_sizes`: sizes sum to 32768, and the largest cohort has exactly 1024 samples. `probs`: the three probabilities of one call are nonnegative and sum to the call's confidence, at most one up to rounding; a missing call has all three zero.
All inputs are finite; a program needn't handle non-finite values.
Results may differ from a plain program's by a relative error of at most 0.0003.
Values may be sent and summed in bfloat16 or wider, within the bound.
No kernel may reach another device: no remote copies, remote signals or barrier semaphores. Data moves between devices by JAX's collectives and lax.ppermute only.
A program may use at most 128 MiB of HBM per device.

v0:
```python
import jax
import jax.numpy as jnp
from jax import lax
from jax.sharding import PartitionSpec as P

REACH = 2


def from_behind(value, axis, steps):
    count = lax.axis_size(axis)
    first, last = (max(0, -steps), min(count, count - steps))
    return lax.ppermute(value, axis, [(source, source + steps) for source in range(first, last)])


def cohort_of(positions, cohort_ends):
    return jnp.sum((cohort_ends[None, :] <= positions[:, None]).astype(jnp.int32), axis=1)


def observed_of(partner_data):
    return (partner_data[0].astype(jnp.float32) + partner_data[1] + partner_data[2]).astype(
        jnp.bfloat16
    )


def left_sides(rows_data):
    rows_obs = observed_of(rows_data)
    left_num = jnp.concatenate([rows_data[1], rows_data[0], rows_data[2]], axis=1)
    left_den = jnp.concatenate([rows_data[1], rows_obs], axis=1)
    return (left_num, left_den)


def pair_counts(left_num, left_den, partner_data):
    partner_obs = observed_of(partner_data)
    right_num = jnp.concatenate(
        [partner_data[1], -2 * partner_data[2], -2 * partner_data[0]], axis=1
    )
    right_den = jnp.concatenate([partner_obs, partner_data[1]], axis=1)
    dims = (((1,), (1,)), ((), ()))
    numerator = lax.dot_general(left_num, right_num, dims, preferred_element_type=jnp.float32)
    denominator = lax.dot_general(left_den, right_den, dims, preferred_element_type=jnp.float32)
    return (numerator, denominator)


def band_of(probs):
    pieces = []
    for offset in range(-REACH, REACH + 1):
        if offset == 0:
            pieces.append(probs)
        else:
            pieces.append(from_behind(probs, "cohort", -offset))
    return jnp.concatenate(pieces, axis=1)


def per_device(probs, cohort_sizes):
    tile_rows = probs.shape[1]
    left_num, left_den = left_sides(probs)
    numerator, denominator = pair_counts(left_num, left_den, band_of(probs))
    num_part, den_part = (
        lax.psum_scatter(numerator, "variant", scatter_dimension=1, tiled=True),
        lax.psum_scatter(denominator, "variant", scatter_dimension=1, tiled=True),
    )
    width = num_part.shape[1]
    block_index = lax.axis_index("cohort")
    samples_total = tile_rows * lax.axis_size("cohort")
    row_pos = block_index * tile_rows + jnp.arange(tile_rows, dtype=jnp.int32)
    col_start = (block_index - REACH) * tile_rows + lax.axis_index("variant") * width
    col_pos = col_start + jnp.arange(width, dtype=jnp.int32)
    inside = (col_pos >= 0) & (col_pos < samples_total)
    cohort_ends = jnp.cumsum(cohort_sizes)
    same_cohort = (
        cohort_of(row_pos, cohort_ends)[:, None] == cohort_of(col_pos, cohort_ends)[None, :]
    )
    ratio = num_part / jnp.maximum(den_part, 1.0)
    return jnp.where(same_cohort & inside[None, :], ratio, 0.0)


def solution(mesh):
    return jax.shard_map(
        per_device,
        mesh=mesh,
        in_specs=(P(None, "cohort", "variant"), P()),
        out_specs=P("cohort", "variant"),
        check_vma=False,
    )
```

profile of v0, /device:TPU:7, one launch (start us, length us, event | category | flops | bytes accessed | tf_op | source)
XLA Modules:
  0.0 268.2 jit_solution(8097129088522400993)
XLA Ops:
  6.5 0.0 reduce-scatter.3.cloned.1.call-start
  6.5 3.5 %collective-permute-start = (bf16[3,512,768]{2,1,0:T(8,128)(2,1)}, bf16[3,512,768]{2,1,0:T(8,128)(2,1)S(1)}, u32[]{:S(2)}, u32[]{:S(2)}) collective-permute-start(bf16[3,512,768]{2,1,0:T(8,128)(2,1)} %param.2), channel_id=1, source_target_pairs={{0,8},{4,12},{8,16},{12,20},{16,24},{20,28},{24,32},{28,36},{32,40... | collective-permute-start | bytes 7077896 | tf_op jit(solution)/shard_map/ppermute | solution.py:12
  10.1 4.8 %collective-permute-start.1 = (bf16[3,512,768]{2,1,0:T(8,128)(2,1)}, bf16[3,512,768]{2,1,0:T(8,128)(2,1)S(1)}, u32[]{:S(2)}, u32[]{:S(2)}) collective-permute-start(bf16[3,512,768]{2,1,0:T(8,128)(2,1)} %param.2), channel_id=1, source_target_pairs={{0,4},{4,8},{8,12},{12,16},{16,20},{20,24},{24,28},{28,32},{32,36}... | collective-permute-start | bytes 7077896 | tf_op jit(solution)/shard_map/ppermute | solution.py:12
  14.9 5.9 %collective-permute-start.2 = (bf16[3,512,768]{2,1,0:T(8,128)(2,1)}, bf16[3,512,768]{2,1,0:T(8,128)(2,1)S(1)}, u32[]{:S(2)}, u32[]{:S(2)}) collective-permute-start(bf16[3,512,768]{2,1,0:T(8,128)(2,1)} %param.2), channel_id=1, source_target_pairs={{4,0},{8,4},{12,8},{16,12},{20,16},{24,20},{28,24},{32,28},{36,32}... | collective-permute-start | bytes 7077896 | tf_op jit(solution)/shard_map/ppermute | solution.py:12
  20.8 3.4 %collective-permute-start.3 = (bf16[3,512,768]{2,1,0:T(8,128)(2,1)}, bf16[3,512,768]{2,1,0:T(8,128)(2,1)S(1)}, u32[]{:S(2)}, u32[]{:S(2)}) collective-permute-start(bf16[3,512,768]{2,1,0:T(8,128)(2,1)} %param.2), channel_id=1, source_target_pairs={{8,0},{12,4},{16,8},{20,12},{24,16},{28,20},{32,24},{36,28},{40,32... | collective-permute-start | bytes 7077896 | tf_op jit(solution)/shard_map/ppermute | solution.py:12
  24.1 2.6 slice_bitcast_fusion.3
  26.8 0.0 copy-start.1
  26.8 38.7 %collective-permute-done = bf16[3,512,768]{2,1,0:T(8,128)(2,1)S(1)} collective-permute-done((bf16[3,512,768]{2,1,0:T(8,128)(2,1)}, bf16[3,512,768]{2,1,0:T(8,128)(2,1)S(1)}, u32[]{:S(2)}, u32[]{:S(2)}) %collective-permute-start) | collective-permute-done | bytes 2359328 | tf_op jit(solution)/shard_map/ppermute | solution.py:12
  65.5 0.2 constant_dynamic-update-slice_fusion.4
  65.6 53.0 %collective-permute-done.1 = bf16[3,512,768]{2,1,0:T(8,128)(2,1)S(1)} collective-permute-done((bf16[3,512,768]{2,1,0:T(8,128)(2,1)}, bf16[3,512,768]{2,1,0:T(8,128)(2,1)S(1)}, u32[]{:S(2)}, u32[]{:S(2)}) %collective-permute-start.1) | collective-permute-done | bytes 2359328 | tf_op jit(solution)/shard_map/ppermute | solution.py:12
  118.6 0.2 constant_dynamic-update-slice_fusion.3
  118.8 0.0 copy-done.1
  118.8 0.2 constant_dynamic-update-slice_fusion.2
  119.0 1.6 collective-permute-done.2
  120.6 0.2 constant_dynamic-update-slice_fusion.1
  120.7 0.8 collective-permute-done.3
  121.5 0.2 constant_dynamic-update-slice_fusion
  121.7 0.0 copy-start
  121.7 3.8 %slice_bitcast_fusion = (bf16[2560,768]{1,0:T(8,128)(2,1)S(1)}, bf16[2560,768]{1,0:T(8,128)(2,1)}, bf16[2560,768]{1,0:T(8,128)(2,1)}) fusion(bf16[3,2560,768]{2,1,0:T(8,128)(2,1)S(1)} %constant_dynamic-update-slice_fusion), kind=kLoop, calls=%fused_computation.13 | loop fusion | flops 3932160 | bytes 23592960 | tf_op jit(solution)/shard_map/squeeze | solution.py:35
  125.5 3.1 %copy-done = bf16[3,2560,768]{2,1,0:T(8,128)(2,1)} copy-done((bf16[3,2560,768]{2,1,0:T(8,128)(2,1)}, bf16[3,2560,768]{2,1,0:T(8,128)(2,1)S(1)}, u32[]{:S(2)}) %copy-start) | copy-done | bytes 11796504
  128.6 0.0 copy-start.2
  128.6 1.8 copy-done.2
  130.5 10.3 %fusion = f32[512,2560]{1,0:T(8,128)} fusion(bf16[2560,768]{1,0:T(8,128)(2,1)} %get-tuple-element.6, bf16[2560,768]{1,0:T(8,128)(2,1)} %get-tuple-element.7, bf16[2560,768]{1,0:T(8,128)(2,1)S(1)} %get-tuple-element.5, bf16[512,768]{1,0:T(8,128)(2,1)S(1)} %get-tuple-element.9, bf16[512,768]{1,0:T(8,128)(2,1)} %get-tuple-element.10, ...), kind=kOutput, calls=%fused_computation | convolution fusion | flops 6082265088 | bytes 19398656 | tf_op jit(solution)/shard_map/dot_general | solution.py:39
  140.8 0.0 reduce-scatter.3.cloned.1.call-update
  140.8 0.0 reduce-scatter.5.cloned.1.call-start
  140.9 0.3 add_convert_fusion
  141.2 0.0 copy-start.3
  141.2 5.3 %fusion.10 = bf16[2560,768]{1,0:T(8,128)(2,1)S(1)} fusion(bf16[3,2560,768]{2,1,0:T(8,128)(2,1)} %copy-done), kind=kLoop, calls=%fused_computation.11 | loop fusion | flops 11796480 | bytes 15728640 | tf_op jit(solution)/shard_map/convert_element_type | solution.py:20
  146.5 0.2 copy-done.3
  146.7 6.0 %fusion.6 = f32[512,2560]{1,0:T(8,128)} fusion(bf16[2560,768]{1,0:T(8,128)(2,1)S(1)} %copy-done.3, bf16[2560,768]{1,0:T(8,128)(2,1)S(1)} %fusion.10, bf16[512,768]{1,0:T(8,128)(2,1)S(1)} %add_convert_fusion, bf16[512,768]{1,0:T(8,128)(2,1)S(1)} %get-tuple-element.8), kind=kOutput, calls=%fused_computation.6 | convolution fusion | flops 4045406208 | bytes 14680064 | tf_op jit(solution)/shard_map/dot_general | solution.py:40
  152.7 0.0 copy-start.4
  152.7 0.0 reduce-scatter.5.cloned.1.call-update
  152.8 0.6 copy-done.4
  153.4 0.1 copy.5
  153.5 0.1 reduce-window.8
  153.6 0.1 reduce
  153.7 0.1 convert_reduce_fusion.1
  153.8 0.1 convert_reduce_fusion
  153.9 44.3 %reduce-scatter.3.cloned.1.call-done = f32[512,640]{1,0:T(8,128)} async-done(((f32[512,2560]{1,0:T(8,128)}), f32[512,640]{1,0:T(8,128)}) %reduce-scatter.3.cloned.1.call-update) | async-done | bytes 1310736 | tf_op jit(solution)/shard_map/reduce_scatter | solution.py:59
  198.2 60.0 %reduce-scatter.5.cloned.1.call-done = f32[512,640]{1,0:T(8,128)} async-done(((f32[512,2560]{1,0:T(8,128)}), f32[512,640]{1,0:T(8,128)}) %reduce-scatter.5.cloned.1.call-update) | async-done | bytes 1310736 | tf_op jit(solution)/shard_map/reduce_scatter | solution.py:60
  258.2 3.1 %divide_select_fusion = f32[512,640]{1,0:T(8,128)} fusion(f32[512,640]{1,0:T(8,128)} %reduce-scatter.3.cloned.1.call-done, f32[512,640]{1,0:T(8,128)} %reduce-scatter.5.cloned.1.call-done, s32[640]{0:T(1024)S(1)} %convert_reduce_fusion, s32[512]{0:T(512)S(1)} %convert_reduce_fusion.1, pred[640]{0:T(1024)(128)(4,1)S(1)} %compare_and_fusion), kind=kLoop, calls=%fused_computation.25 | loop fusion | flops 1638400 | bytes 3937408 | tf_op jit(solution)/shard_map/jit(_where)/select_n | solution.py:74
  (3 shorter events, 0.0 us)
Async XLA Ops:
  6.5 191.7 %reduce-scatter.3.cloned.1.call-start = ((), (), s32[]{:S(2)}) async-start(), calls=%async_computation.2 | async-start | bytes 6553600 | tf_op jit(solution)/shard_map/reduce_scatter | solution.py:59
  6.5 58.9 %collective-permute-start = (bf16[3,512,768]{2,1,0:T(8,128)(2,1)}, bf16[3,512,768]{2,1,0:T(8,128)(2,1)S(1)}, u32[]{:S(2)}, u32[]{:S(2)}) collective-permute-start(bf16[3,512,768]{2,1,0:T(8,128)(2,1)} %param.2), channel_id=1, source_target_pairs={{0,8},{4,12},{8,16},{12,20},{16,24},{20,28},{24,32},{28,36},{32,40... | collective-permute-start | bytes 7077896 | tf_op jit(solution)/shard_map/ppermute | solution.py:12
  10.1 108.6 %collective-permute-start.1 = (bf16[3,512,768]{2,1,0:T(8,128)(2,1)}, bf16[3,512,768]{2,1,0:T(8,128)(2,1)S(1)}, u32[]{:S(2)}, u32[]{:S(2)}) collective-permute-start(bf16[3,512,768]{2,1,0:T(8,128)(2,1)} %param.2), channel_id=1, source_target_pairs={{0,4},{4,8},{8,12},{12,16},{16,20},{20,24},{24,28},{28,32},{32,36}... | collective-permute-start | bytes 7077896 | tf_op jit(solution)/shard_map/ppermute | solution.py:12
  14.9 105.7 %collective-permute-start.2 = (bf16[3,512,768]{2,1,0:T(8,128)(2,1)}, bf16[3,512,768]{2,1,0:T(8,128)(2,1)S(1)}, u32[]{:S(2)}, u32[]{:S(2)}) collective-permute-start(bf16[3,512,768]{2,1,0:T(8,128)(2,1)} %param.2), channel_id=1, source_target_pairs={{4,0},{8,4},{12,8},{16,12},{20,16},{24,20},{28,24},{32,28},{36,32}... | collective-permute-start | bytes 7077896 | tf_op jit(solution)/shard_map/ppermute | solution.py:12
  20.8 100.8 %collective-permute-start.3 = (bf16[3,512,768]{2,1,0:T(8,128)(2,1)}, bf16[3,512,768]{2,1,0:T(8,128)(2,1)S(1)}, u32[]{:S(2)}, u32[]{:S(2)}) collective-permute-start(bf16[3,512,768]{2,1,0:T(8,128)(2,1)} %param.2), channel_id=1, source_target_pairs={{8,0},{12,4},{16,8},{20,12},{24,16},{28,20},{32,24},{36,28},{40,32... | collective-permute-start | bytes 7077896 | tf_op jit(solution)/shard_map/ppermute | solution.py:12
  26.8 92.0 %copy-start.1 = (bf16[3,512,768]{2,1,0:T(8,128)(2,1)S(1)}, bf16[3,512,768]{2,1,0:T(8,128)(2,1)}, u32[]{:S(2)}) copy-start(bf16[3,512,768]{2,1,0:T(8,128)(2,1)} %param.2) | copy-start | bytes 7077892
  121.7 6.9 %copy-start = (bf16[3,2560,768]{2,1,0:T(8,128)(2,1)}, bf16[3,2560,768]{2,1,0:T(8,128)(2,1)S(1)}, u32[]{:S(2)}) copy-start(bf16[3,2560,768]{2,1,0:T(8,128)(2,1)S(1)} %constant_dynamic-update-slice_fusion) | copy-start | bytes 35389444
  128.6 1.8 copy-start.2
  140.8 117.4 %reduce-scatter.5.cloned.1.call-start = ((), (), s32[]{:S(2)}) async-start(), calls=%async_computation.3 | async-start | bytes 6553600 | tf_op jit(solution)/shard_map/reduce_scatter | solution.py:60
  141.2 5.5 %copy-start.3 = (bf16[2560,768]{1,0:T(8,128)(2,1)S(1)}, bf16[2560,768]{1,0:T(8,128)(2,1)}, u32[]{:S(2)}) copy-start(bf16[2560,768]{1,0:T(8,128)(2,1)} %copy-done.2) | copy-start | bytes 11796484
  152.7 0.7 copy-start.4
Sparse Core Ops, SparseCore 0:
  141.0 57.2 reduce-scatter.2
  200.8 57.3 reduce-scatter.4
where the time goes:
time: 269 us; the launch traced here: 268 us
  waiting for transfers between devices  198 us (74%)
  starting transfers between devices  17.6 us (7%)
  matrix products  16.3 us (6%)
  between operations  13.6 us (5%)
  other arithmetic  12.9 us (5%)
  local copies, waits for them, and re-layouts  9.34 us (3%)
    ppermute x4, waiting for transfers between devices, from_behind(): lax.ppermute(value, axis, [(source, source + steps) for source in range(f...  94.1 us
    reduce_scatter x1, waiting for transfers between devices, per_device(): lax.psum_scatter(denominator, 'variant', scatter_dimension=1, tiled=True)  60 us
    reduce_scatter x1, waiting for transfers between devices, per_device(): lax.psum_scatter(numerator, 'variant', scatter_dimension=1, tiled=True)  44.3 us
    ppermute x4, starting transfers between devices, from_behind(): lax.ppermute(value, axis, [(source, source + steps) for source in range(f...  17.6 us
    dot_general x1, matrix products, pair_counts(): lax.dot_general(left_num, right_num, dims, preferred_element_type=jnp.flo...  10.3 us
    unnamed x14, local copies, waits for them, and re-layouts  6.44 us
    dot_general x1, matrix products, pair_counts(): lax.dot_general(left_den, right_den, dims, preferred_element_type=jnp.flo...  6 us
    convert_element_type x2, other arithmetic, observed_of(): (partner_data[0].astype(jnp.float32) + partner_data[1] + partner_data[2])...  5.57 us
  transfers between devices with their start and end apart: 6, of which 6 were waited for; matrix products, arithmetic and copies ran while one was open for 6% of the time, Pallas kernels for 0%

commit v1 on v0

v1 whole, which is shorter than its diff:
```python
import jax
import jax.numpy as jnp
from jax import lax
from jax.experimental import pallas as pl
from jax.experimental.pallas import tpu as pltpu
from jax.sharding import PartitionSpec as P

AXES = ("cohort", "variant")
TILE = 512
HALF = 256
WIDTH = 640
F32 = jnp.float32


def route(blocks, rule):
    pairs = []
    for k in range(blocks // 2):
        for par in range(2):
            for lo in range(2):
                for core in range(2):
                    to = rule(k, par, lo, core)
                    if to is not None and 0 <= to[0] < blocks // 2:
                        source = (2 * k + par) * 4 + lo * 2 + core
                        pairs.append((source, (2 * to[0] + to[1]) * 4 + to[2] * 2 + to[3]))
    return pairs


def is_a(par, core):
    return core == par


def is_outer(par, lo):
    return lo == par


def to_mate(k, par, lo, core):
    if is_a(par, core):
        return (k, par, lo, 1 - core)
    return (k, 1 - par, lo, core)


def to_next(k, par, lo, core):
    return (k - 1 if core == 0 else k + 1, par, lo, core)


def to_chip(k, par, lo, core):
    return (k, par, 1 - lo, core)


def to_chip_a(k, par, lo, core):
    return (k, par, 1 - lo, core) if is_a(par, core) else None


def to_far(k, par, lo, core):
    return (k + 1 if core == 0 else k - 1, par, lo, 1 - core)


def to_mirror(k, par, lo, core):
    return (k, 1 - par, 1 - lo, 1 - core) if is_a(par, core) else None


def to_cut(k, par, lo, core):
    if is_a(par, core) and is_outer(par, lo):
        return (k + 1 if par == 0 else k - 1, par, lo, core)
    return None


def to_owner(k, par, lo, core):
    if is_a(par, core) == is_outer(par, lo):
        return (k, par, 1 - lo, core)
    return None


def to_core(k, par, lo, core):
    return (k, par, lo, 1 - core)


def dot_t(left, right):
    return lax.dot_general(left, right, (((1,), (1,)), ((), ())), preferred_element_type=F32)


def pair_sums(left, left_obs, right, right_obs):
    cross = dot_t(left[0], right[2]) + dot_t(left[2], right[0])
    num = dot_t(left[1], right[1]) - 2.0 * cross
    den = dot_t(left[1], right_obs[...]) + dot_t(left_obs[...], right[1])
    return num, den


def sums_kernel(role, own, mate, far, send_a, send_b, keep_a, keep_b, tri, own_obs, mate_obs, far_obs):
    par, lo, core = role[0], role[1], role[2]
    kind_a = core == par
    outer = lo == par
    for source, target in ((own, own_obs), (mate, mate_obs), (far, far_obs)):
        total = source[0].astype(F32) + source[1].astype(F32) + source[2].astype(F32)
        target[...] = total.astype(jnp.bfloat16)

    def put(first, second, values):
        for i in range(2):
            first[i] = values[i][:, :HALF]
            second[i] = values[i][:, HALF:]

    @pl.when(kind_a)
    def _():
        near = pair_sums(own, own_obs, mate, mate_obs)

        @pl.when(outer)
        def _():
            put(send_a, send_b, near)

        @pl.when(jnp.logical_not(outer))
        def _():
            put(keep_a, keep_b, near)

        cut = pair_sums(mate, mate_obs, far, far_obs)

        @pl.when(outer)
        def _():
            put(keep_a, keep_b, cut)

        @pl.when(jnp.logical_not(outer))
        def _():
            put(send_a, send_b, cut)

        both = pair_sums(own, own_obs, far, far_obs)
        tri[0] = both[0]
        tri[1] = both[1]

    @pl.when(jnp.logical_not(kind_a))
    def _():
        first = pair_sums(own, own_obs, own, own_obs)
        second = pair_sums(mate, mate_obs, mate, mate_obs)
        diag = (first[0] + second[0], first[1] + second[1])

        @pl.when(lo == 0)
        def _():
            put(keep_a, send_a, diag)

        @pl.when(lo == 1)
        def _():
            put(send_a, keep_a, diag)

        both = pair_sums(far, far_obs, own, own_obs)
        tri[0] = both[0]
        tri[1] = both[1]


def ratio(num, den):
    return num / jnp.maximum(den, 1.0)


def ratio_kernel(role, half_sum, full_a, full_b, mirror_a, mirror_b, cut_a, cut_b, tri, tri_in, send, keep):
    par, lo, core = role[0], role[1], role[2]
    kind_a = core == par
    outer = lo == par
    even = par == 0

    def joined(first, second, i):
        return jnp.concatenate([first[i], second[i]], axis=1)

    @pl.when(kind_a & outer)
    def _():
        num = joined(mirror_a, mirror_b, 0) + joined(cut_a, cut_b, 0).T
        den = joined(mirror_a, mirror_b, 1) + joined(cut_a, cut_b, 1).T
        value = ratio(num, den)

        @pl.when(even)
        def _():
            keep[:, :128] = value[:, :128]
            send[:, :384] = value[:, 128:]

        @pl.when(jnp.logical_not(even))
        def _():
            keep[:, :128] = value[:, 384:]
            send[:, :384] = value[:, :384]

    @pl.when(kind_a & jnp.logical_not(outer))
    def _():
        num = joined(full_a, full_b, 0) + joined(mirror_a, mirror_b, 0).T
        den = joined(full_a, full_b, 1) + joined(mirror_a, mirror_b, 1).T
        value = ratio(num, den)
        beyond = ratio(tri[0] + tri_in[0], tri[1] + tri_in[1])

        @pl.when(even)
        def _():
            keep[:, :384] = value[:, :384]
            send[:, :128] = value[:, 384:]
            send[:, 128:] = beyond

        @pl.when(jnp.logical_not(even))
        def _():
            keep[:, :384] = value[:, 128:]
            send[:, 512:] = value[:, :128]
            send[:, :512] = beyond

    @pl.when(jnp.logical_not(kind_a) & outer)
    def _():
        send[:, :512] = ratio(tri[0] + tri_in[0], tri[1] + tri_in[1]).T
        keep[:, :256] = ratio(half_sum[0], half_sum[1])

    @pl.when(jnp.logical_not(kind_a) & jnp.logical_not(outer))
    def _():
        send[:, :256] = ratio(half_sum[0], half_sum[1])


def place_kernel(role, row_cohort, col_cohort, keep, came, out):
    par, lo, core = role[0], role[1], role[2]
    kind_a = core == par
    outer = lo == par
    rows = row_cohort[...]

    def put(start, value):
        width = value.shape[1]
        same = rows == col_cohort[:, start : start + width]
        out[:, start : start + width] = jnp.where(same, value, 0.0)

    def one(parity, far_kind, outer_kind, parts):
        want = (par == parity) & (kind_a == far_kind) & (outer == outer_kind)

        @pl.when(want)
        def _():
            start = 0
            for ref, width in parts:
                put(start, ref[:, :width])
                start += width

    one(0, True, True, [(came, 512), (keep, 128)])
    one(0, False, True, [(came, 384), (keep, 256)])
    one(0, True, False, [(came, 256), (keep, 384)])
    one(0, False, False, [(came, 640)])
    one(1, False, False, [(came, 640)])
    one(1, True, False, [(keep, 384), (came, 256)])
    one(1, False, True, [(keep, 256), (came, 384)])
    one(1, True, True, [(keep, 128), (came, 512)])


def cohort_of(positions, cohort_ends):
    return jnp.sum((cohort_ends[None, :] <= positions[:, None]).astype(jnp.int32), axis=1)


def call(kernel, out_shapes, in_count, scratch=()):
    vmem = pl.BlockSpec(memory_space=pltpu.VMEM)
    return pl.pallas_call(
        kernel,
        out_shape=out_shapes,
        in_specs=[pl.BlockSpec(memory_space=pltpu.SMEM)] + [vmem] * in_count,
        out_specs=jax.tree.map(lambda _: vmem, out_shapes),
        scratch_shapes=list(scratch),
        compiler_params=pltpu.CompilerParams(vmem_limit_bytes=50 * 1024 * 1024),
    )


def per_device(probs, cohort_sizes):
    blocks = lax.axis_size("cohort")
    block = lax.axis_index("cohort")
    quarter = lax.axis_index("variant")
    role = jnp.stack([block % 2, quarter // 2, quarter % 2]).astype(jnp.int32)

    def move(value, rule):
        return lax.ppermute(value, AXES, route(blocks, rule))

    mate = move(probs, to_mate)
    far = move(probs, to_next)
    half = jax.ShapeDtypeStruct((2, TILE, HALF), F32)
    full = jax.ShapeDtypeStruct((2, TILE, TILE), F32)
    obs = pltpu.VMEM(probs.shape[1:], jnp.bfloat16)
    send_a, send_b, keep_a, keep_b, tri = call(
        sums_kernel, (half, half, half, half, full), 3, (obs, obs, obs)
    )(role, probs, mate, far)
    full_a = keep_a + move(send_a, to_chip)
    tri = tri + move(tri, to_far)
    full_b = keep_b + move(send_b, to_chip_a)
    mirror_a = move(full_a, to_mirror)
    cut_a = move(full_a, to_cut)
    tri_in = move(tri, to_owner)
    mirror_b = move(full_b, to_mirror)
    cut_b = move(full_b, to_cut)
    wide = jax.ShapeDtypeStruct((TILE, WIDTH), F32)
    narrow = jax.ShapeDtypeStruct((TILE, 384), F32)
    send, keep = call(ratio_kernel, (wide, narrow), 9)(
        role, full_a, full_a, full_b, mirror_a, mirror_b, cut_a, cut_b, tri, tri_in
    )
    came = move(send, to_core)

    cohort_ends = jnp.cumsum(cohort_sizes)
    row_pos = block * TILE + jnp.arange(TILE, dtype=jnp.int32)
    col_pos = (block - 2) * TILE + quarter * WIDTH + jnp.arange(WIDTH, dtype=jnp.int32)
    inside = (col_pos >= 0) & (col_pos < TILE * blocks)
    row_cohort = cohort_of(row_pos, cohort_ends)[:, None]
    col_cohort = jnp.where(inside, cohort_of(col_pos, cohort_ends), -1)[None, :]
    return call(place_kernel, wide, 4)(role, row_cohort, col_cohort, keep, came)


def solution(mesh):
    return jax.shard_map(
        per_device,
        mesh=mesh,
        in_specs=(P(None, "cohort", "variant"), P()),
        out_specs=P("cohort", "variant"),
        check_vma=False,
    )
```

time: 269 us -> 132 us (0.49)
  waiting for transfers between devices: 198 us -> 80.8 us
  Pallas kernels: 0 us -> 18.7 us
  matrix products: 16.3 us -> 0 us
  between operations: 13.6 us -> 0.28 us
  other arithmetic: 12.9 us -> 2.8 us
  starting transfers between devices: 17.6 us -> 25.6 us
  local copies, waits for them, and re-layouts: 9.34 us -> 1.59 us
    reduce_scatter x2 -> x0, waiting for transfers between devices: 104 us -> none  [the longest x1 60 us: per_device(): lax.psum_scatter(denominator, 'variant', scatter_dimension=1, tiled=True)]
    pallas_call x0 -> x3, Pallas kernels: none -> 18.7 us  [the longest x1 12.2 us: per_device(): call(sums_kernel, (half, half, half, half, full), 3, (obs, obs, obs))]
    dot_general x2 -> x0, matrix products: 16.3 us -> none  [the longest x1 10.3 us: pair_counts(): lax.dot_general(left_num, right_num, dims, preferred_element_type=jnp.flo...]
    ppermute x4 -> x11, waiting for transfers between devices: 94.1 us -> 80.8 us  [move(): return lax.ppermute(value, AXES, route(blocks, rule))]
    ppermute x4 -> x11, starting transfers between devices: 17.6 us -> 25.6 us  [move(): return lax.ppermute(value, AXES, route(blocks, rule))]
    convert_element_type x2 -> x0, other arithmetic: 5.57 us -> none  [observed_of(): (partner_data[0].astype(jnp.float32) + partner_data[1] + partner_data[2])...]
    unnamed x14 -> x16, local copies, waits for them, and re-layouts: 6.44 us -> 1.34 us
    squeeze x1 -> x0, other arithmetic: 3.8 us -> none  [pair_counts(): partner_data[1]]
  transfers between devices with their start and end apart: 6 -> 11, of which waited for: 6 -> 5; matrix products, arithmetic and copies ran while one was open for 6% -> 2% of each run, Pallas kernels for 0% -> 0%
where the time goes in v1:
time: 132 us; the launch traced here: 130 us
  waiting for transfers between devices  80.8 us (61%)
  starting transfers between devices  25.6 us (19%)
  Pallas kernels  18.7 us (14%)
  other arithmetic  2.8 us (2%)
  local copies, waits for them, and re-layouts  1.59 us (1%)
    ppermute x11, waiting for transfers between devices, move(): return lax.ppermute(value, AXES, route(blocks, rule))  80.8 us
    ppermute x11, starting transfers between devices, move(): return lax.ppermute(value, AXES, route(blocks, rule))  25.6 us
    pallas_call x1, Pallas kernels, per_device(): call(sums_kernel, (half, half, half, half, full), 3, (obs, obs, obs))  12.2 us
    pallas_call x1, Pallas kernels, per_device(): call(ratio_kernel, (wide, narrow), 9)  4.62 us
  transfers between devices with their start and end apart: 11, of which 5 were waited for; matrix products, arithmetic and copies ran while one was open for 2% of the time, Pallas kernels for 0%

profile of v1, /device:TPU:7, one launch (start us, length us, event | category | flops | bytes accessed | tf_op | source)
XLA Modules:
  0.0 129.7 jit_solution(14055090739416758776)
XLA Ops:
  0.0 2.9 %collective-permute-start = (bf16[3,512,768]{2,1,0:T(8,128)(2,1)}, bf16[3,512,768]{2,1,0:T(8,128)(2,1)S(1)}, u32[]{:S(2)}, u32[]{:S(2)}) collective-permute-start(bf16[3,512,768]{2,1,0:T(8,128)(2,1)} %own.1), channel_id=1, source_target_pairs={{0,1},{1,5},{2,3},{3,7},{4,0},{5,4},{6,2},{7,6},{8,9},{9,13},{10,1... | collective-permute-start | bytes 7077896 | tf_op jit(solution)/shard_map/ppermute | solution.py:259
  2.9 3.5 %collective-permute-start.1 = (bf16[3,512,768]{2,1,0:T(8,128)(2,1)}, bf16[3,512,768]{2,1,0:T(8,128)(2,1)}, u32[]{:S(2)}, u32[]{:S(2)}) collective-permute-start(bf16[3,512,768]{2,1,0:T(8,128)(2,1)} %own.1), channel_id=1, source_target_pairs={{1,9},{3,11},{5,13},{7,15},{8,0},{9,17},{10,2},{11,19},{12,4},{13,... | collective-permute-start | bytes 7077896 | tf_op jit(solution)/shard_map/ppermute | solution.py:259
  6.5 0.1 pad_add_fusion.role
  6.6 22.5 %collective-permute-done.mate = bf16[3,512,768]{2,1,0:T(8,128)(2,1)S(1)} collective-permute-done((bf16[3,512,768]{2,1,0:T(8,128)(2,1)}, bf16[3,512,768]{2,1,0:T(8,128)(2,1)S(1)}, u32[]{:S(2)}, u32[]{:S(2)}) %collective-permute-start) | collective-permute-done | bytes 2359328 | tf_op jit(solution)/shard_map/ppermute | solution.py:259
  29.0 0.0 copy-start.1
  29.0 8.2 %collective-permute-done.1.far = bf16[3,512,768]{2,1,0:T(8,128)(2,1)} collective-permute-done((bf16[3,512,768]{2,1,0:T(8,128)(2,1)}, bf16[3,512,768]{2,1,0:T(8,128)(2,1)}, u32[]{:S(2)}, u32[]{:S(2)}) %collective-permute-start.1) | collective-permute-done | bytes 2359328 | tf_op jit(solution)/shard_map/ppermute | solution.py:259
  37.2 0.0 copy-done.1
  37.2 12.2 %shard_map.28 = (f32[2,512,256]{2,1,0:T(8,128)S(1)}, f32[2,512,256]{2,1,0:T(8,128)S(1)}, f32[2,512,256]{2,1,0:T(8,128)S(1)}, f32[2,512,256]{2,1,0:T(8,128)}, f32[2,512,512]{2,1,0:T(8,128)}) custom-call(s32[3]{0:T(128)S(1)} %pad_add_fusion.role, bf16[3,512,768]{2,1,0:T(8,128)(2,1)} %own.1, bf16[3,512,768]{2,1,0:T(8,128)(2,1)} %copy-done.1, ...), custom_call_target="tpu_custom_call" | custom-call | tf_op jit(solution)/shard_map/pallas_call | solution.py:266
  49.4 4.6 %collective-permute-start.8 = (f32[2,512,512]{2,1,0:T(8,128)}, f32[2,512,512]{2,1,0:T(8,128)S(1)}, u32[]{:S(2)}, u32[]{:S(2)}) collective-permute-start(f32[2,512,512]{2,1,0:T(8,128)} %get-tuple-element.16), channel_id=1, source_target_pairs={{0,9},{2,11},{4,13},{6,15},{8,17},{9,0},{10,19},{11,2},{12,21},{13... | collective-permute-start | bytes 6291464 | tf_op jit(solution)/shard_map/ppermute | solution.py:259
  54.0 0.7 collective-permute-start.3
  54.8 0.0 copy-start.5
  54.8 1.6 %collective-permute-start.2 = (f32[2,512,256]{2,1,0:T(8,128)S(1)}, f32[2,512,256]{2,1,0:T(8,128)S(1)}, u32[]{:S(2)}, u32[]{:S(2)}) collective-permute-start(f32[2,512,256]{2,1,0:T(8,128)S(1)} %get-tuple-element.13), channel_id=1, source_target_pairs={{0,2},{1,3},{2,0},{3,1},{4,6},{5,7},{6,4},{7,5},{8,10},{9,11},{10,... | collective-permute-start | bytes 3145736 | tf_op jit(solution)/shard_map/ppermute | solution.py:259
  56.4 22.7 %collective-permute-done.8 = f32[2,512,512]{2,1,0:T(8,128)S(1)} collective-permute-done((f32[2,512,512]{2,1,0:T(8,128)}, f32[2,512,512]{2,1,0:T(8,128)S(1)}, u32[]{:S(2)}, u32[]{:S(2)}) %collective-permute-start.8) | collective-permute-done | bytes 2097184 | tf_op jit(solution)/shard_map/ppermute | solution.py:259
  79.1 2.1 %add.63.tri = f32[2,512,512]{2,1,0:T(8,128)S(1)} add(f32[2,512,512]{2,1,0:T(8,128)} %get-tuple-element.16, f32[2,512,512]{2,1,0:T(8,128)S(1)} %collective-permute-done.8) | non-fusion elementwise | flops 524288 | bytes 6291456 | tf_op jit(solution)/shard_map/add | solution.py:270
  81.2 0.0 copy-start
  81.2 1.3 collective-permute-start.9
  82.5 0.0 collective-permute-done.3
  82.5 0.0 copy-done.5
  82.5 0.1 add.62.full_b
  82.6 0.7 collective-permute-start.5
  83.4 0.7 collective-permute-start.7
  84.1 0.0 collective-permute-done.2
  84.1 0.1 add.61.half_sum.full_a
  84.3 0.0 copy-done
  84.3 0.0 copy-start.7
  84.3 0.7 collective-permute-start.4
  85.0 0.7 collective-permute-start.6
  85.8 0.0 collective-permute-done.5.mirror_b
  85.8 0.0 copy-start.3
  85.8 0.0 collective-permute-done.7.cut_b
  85.8 0.0 copy-start.4
  85.8 0.0 collective-permute-done.4.mirror_a
  85.8 0.0 collective-permute-done.6.cut_a
  85.8 0.0 copy-start.6
  85.8 25.3 %collective-permute-done.9.tri_in = f32[2,512,512]{2,1,0:T(8,128)S(1)} collective-permute-done((f32[2,512,512]{2,1,0:T(8,128)S(1)}, f32[2,512,512]{2,1,0:T(8,128)S(1)}, u32[]{:S(2)}, u32[]{:S(2)}) %collective-permute-start.9) | collective-permute-done | bytes 2097184 | tf_op jit(solution)/shard_map/ppermute | solution.py:259
  111.1 0.0 copy-done.3
  111.1 0.0 copy-done.4
  111.1 0.0 copy-done.6
  111.1 0.0 copy-start.2
  111.1 1.3 %copy-done.2 = f32[2,512,512]{2,1,0:T(8,128)} copy-done((f32[2,512,512]{2,1,0:T(8,128)}, f32[2,512,512]{2,1,0:T(8,128)S(1)}, u32[]{:S(2)}) %copy-start.2) | copy-done | bytes 2097176
  112.4 4.6 %shard_map.29 = (f32[512,640]{1,0:T(8,128)}, f32[512,384]{1,0:T(8,128)S(1)}) custom-call(s32[3]{0:T(128)S(1)} %pad_add_fusion.role, f32[2,512,256]{2,1,0:T(8,128)S(1)} %add.61.half_sum.full_a, f32[2,512,256]{2,1,0:T(8,128)S(1)} %add.61.half_sum.full_a, f32[2,512,256]{2,1,0:T(8,128)S(1)} %add.62.full_b, f32[2,512,256]{2,1,0:T(8,128)S(1)} %collective-permute-done.4.mirror_a, ...), custom_call_target="tpu_custom_call" | custom-call | tf_op jit(solution)/shard_map/pallas_call | solution.py:279
  117.0 8.0 %collective-permute-start.10 = (f32[512,640]{1,0:T(8,128)}, f32[512,640]{1,0:T(8,128)S(1)}, u32[]{:S(2)}, u32[]{:S(2)}) collective-permute-start(f32[512,640]{1,0:T(8,128)} %get-tuple-element.18), channel_id=1, source_target_pairs={{0,1},{1,0},{2,3},{3,2},{4,5},{5,4},{6,7},{7,6},{8,9},{9,8},{10,11... | collective-permute-start | bytes 3932168 | tf_op jit(solution)/shard_map/ppermute | solution.py:259
  125.1 0.0 copy-done.7
  125.1 0.1 copy.6
  125.2 0.1 reduce-window.8
  125.2 0.1 reduce
  125.4 0.1 convert_reduce_fusion.1
  125.5 0.1 copy.7.row_cohort
  125.6 0.1 convert_reduce_fusion
  125.7 2.2 %collective-permute-done.10.came = f32[512,640]{1,0:T(8,128)S(1)} collective-permute-done((f32[512,640]{1,0:T(8,128)}, f32[512,640]{1,0:T(8,128)S(1)}, u32[]{:S(2)}, u32[]{:S(2)}) %collective-permute-start.10) | collective-permute-done | bytes 1310752 | tf_op jit(solution)/shard_map/ppermute | solution.py:259
  127.9 1.8 %shard_map.30 = f32[512,640]{1,0:T(8,128)} custom-call(s32[3]{0:T(128)S(1)} %pad_add_fusion.role, s32[512,1]{1,0:T(8,128)S(1)} %copy.7.row_cohort, s32[1,640]{1,0:T(1,128)S(1)} %and_select_fusion.col_cohort, f32[512,384]{1,0:T(8,128)S(1)} %get-tuple-element.17.keep, f32[512,640]{1,0:T(8,128)S(1)} %collective-permute-done.10.came), custom_call_target="tpu_custom_call" | custom-call | tf_op jit(solution)/shard_map/pallas_call | solution.py:290
  (3 shorter events, 0.0 us)
Async XLA Ops:
  0.0 29.0 %collective-permute-start = (bf16[3,512,768]{2,1,0:T(8,128)(2,1)}, bf16[3,512,768]{2,1,0:T(8,128)(2,1)S(1)}, u32[]{:S(2)}, u32[]{:S(2)}) collective-permute-start(bf16[3,512,768]{2,1,0:T(8,128)(2,1)} %own.1), channel_id=1, source_target_pairs={{0,1},{1,5},{2,3},{3,7},{4,0},{5,4},{6,2},{7,6},{8,9},{9,13},{10,1... | collective-permute-start | bytes 7077896 | tf_op jit(solution)/shard_map/ppermute | solution.py:259
  2.9 34.3 %collective-permute-start.1 = (bf16[3,512,768]{2,1,0:T(8,128)(2,1)}, bf16[3,512,768]{2,1,0:T(8,128)(2,1)}, u32[]{:S(2)}, u32[]{:S(2)}) collective-permute-start(bf16[3,512,768]{2,1,0:T(8,128)(2,1)} %own.1), channel_id=1, source_target_pairs={{1,9},{3,11},{5,13},{7,15},{8,0},{9,17},{10,2},{11,19},{12,4},{13,... | collective-permute-start | bytes 7077896 | tf_op jit(solution)/shard_map/ppermute | solution.py:259
  29.0 8.2 %copy-start.1 = (bf16[3,512,768]{2,1,0:T(8,128)(2,1)}, bf16[3,512,768]{2,1,0:T(8,128)(2,1)S(1)}, u32[]{:S(2)}) copy-start(bf16[3,512,768]{2,1,0:T(8,128)(2,1)S(1)} %collective-permute-done.mate) | copy-start | bytes 7077892
  49.4 29.7 %collective-permute-start.8 = (f32[2,512,512]{2,1,0:T(8,128)}, f32[2,512,512]{2,1,0:T(8,128)S(1)}, u32[]{:S(2)}, u32[]{:S(2)}) collective-permute-start(f32[2,512,512]{2,1,0:T(8,128)} %get-tuple-element.16), channel_id=1, source_target_pairs={{0,9},{2,11},{4,13},{6,15},{8,17},{9,0},{10,19},{11,2},{12,21},{13... | collective-permute-start | bytes 6291464 | tf_op jit(solution)/shard_map/ppermute | solution.py:259
  54.0 28.4 %collective-permute-start.3 = (f32[2,512,256]{2,1,0:T(8,128)S(1)}, f32[2,512,256]{2,1,0:T(8,128)S(1)}, u32[]{:S(2)}, u32[]{:S(2)}) collective-permute-start(f32[2,512,256]{2,1,0:T(8,128)S(1)} %get-tuple-element.15), channel_id=1, source_target_pairs={{0,2},{2,0},{5,7},{7,5},{8,10},{10,8},{13,15},{15,13},{16,18},{18,... | collective-permute-start | bytes 3145736 | tf_op jit(solution)/shard_map/ppermute | solution.py:259
  54.8 27.7 %copy-start.5 = (f32[2,512,256]{2,1,0:T(8,128)S(1)}, f32[2,512,256]{2,1,0:T(8,128)}, u32[]{:S(2)}) copy-start(f32[2,512,256]{2,1,0:T(8,128)} %get-tuple-element.14) | copy-start | bytes 3145732
  54.8 29.3 %collective-permute-start.2 = (f32[2,512,256]{2,1,0:T(8,128)S(1)}, f32[2,512,256]{2,1,0:T(8,128)S(1)}, u32[]{:S(2)}, u32[]{:S(2)}) collective-permute-start(f32[2,512,256]{2,1,0:T(8,128)S(1)} %get-tuple-element.13), channel_id=1, source_target_pairs={{0,2},{1,3},{2,0},{3,1},{4,6},{5,7},{6,4},{7,5},{8,10},{9,11},{10,... | collective-permute-start | bytes 3145736 | tf_op jit(solution)/shard_map/ppermute | solution.py:259
  81.2 3.1 %copy-start = (f32[2,512,512]{2,1,0:T(8,128)}, f32[2,512,512]{2,1,0:T(8,128)S(1)}, u32[]{:S(2)}) copy-start(f32[2,512,512]{2,1,0:T(8,128)S(1)} %add.63.tri) | copy-start | bytes 6291460
  81.2 29.9 %collective-permute-start.9 = (f32[2,512,512]{2,1,0:T(8,128)S(1)}, f32[2,512,512]{2,1,0:T(8,128)S(1)}, u32[]{:S(2)}, u32[]{:S(2)}) collective-permute-start(f32[2,512,512]{2,1,0:T(8,128)S(1)} %add.63.tri), channel_id=1, source_target_pairs={{0,2},{3,1},{4,6},{7,5},{8,10},{11,9},{12,14},{15,13},{16,18},{19,... | collective-permute-start | bytes 6291464 | tf_op jit(solution)/shard_map/ppermute | solution.py:259
  82.6 3.1 %collective-permute-start.5 = (f32[2,512,256]{2,1,0:T(8,128)S(1)}, f32[2,512,256]{2,1,0:T(8,128)S(1)}, u32[]{:S(2)}, u32[]{:S(2)}) collective-permute-start(f32[2,512,256]{2,1,0:T(8,128)S(1)} %add.62.full_b), channel_id=1, source_target_pairs={{0,7},{2,5},{5,2},{7,0},{8,15},{10,13},{13,10},{15,8},{16,23},{18,... | collective-permute-start | bytes 3145736 | tf_op jit(solution)/shard_map/ppermute | solution.py:259
  83.4 2.4 %collective-permute-start.7 = (f32[2,512,256]{2,1,0:T(8,128)S(1)}, f32[2,512,256]{2,1,0:T(8,128)S(1)}, u32[]{:S(2)}, u32[]{:S(2)}) collective-permute-start(f32[2,512,256]{2,1,0:T(8,128)S(1)} %add.62.full_b), channel_id=1, source_target_pairs={{0,8},{8,16},{15,7},{16,24},{23,15},{24,32},{31,23},{32,40},{39,31... | collective-permute-start | bytes 3145736 | tf_op jit(solution)/shard_map/ppermute | solution.py:259
  84.3 40.8 %copy-start.7 = (s32[42]{0:T(128)S(1)}, s32[42]{0:T(128)}, u32[]{:S(2)}) copy-start(s32[42]{0:T(128)} %param.3) | copy-start | bytes 508
  84.3 1.5 %collective-permute-start.4 = (f32[2,512,256]{2,1,0:T(8,128)S(1)}, f32[2,512,256]{2,1,0:T(8,128)S(1)}, u32[]{:S(2)}, u32[]{:S(2)}) collective-permute-start(f32[2,512,256]{2,1,0:T(8,128)S(1)} %add.61.half_sum.full_a), channel_id=1, source_target_pairs={{0,7},{2,5},{5,2},{7,0},{8,15},{10,13},{13,10},{15,8},{16,23},{18,... | collective-permute-start | bytes 3145736 | tf_op jit(solution)/shard_map/ppermute | solution.py:259
  85.0 0.8 collective-permute-start.6
  85.8 25.3 %copy-start.3 = (f32[2,512,256]{2,1,0:T(8,128)}, f32[2,512,256]{2,1,0:T(8,128)S(1)}, u32[]{:S(2)}) copy-start(f32[2,512,256]{2,1,0:T(8,128)S(1)} %collective-permute-done.5.mirror_b) | copy-start | bytes 3145732
  85.8 25.3 %copy-start.4 = (f32[2,512,256]{2,1,0:T(8,128)}, f32[2,512,256]{2,1,0:T(8,128)S(1)}, u32[]{:S(2)}) copy-start(f32[2,512,256]{2,1,0:T(8,128)S(1)} %collective-permute-done.7.cut_b) | copy-start | bytes 3145732
  85.8 25.3 %copy-start.6 = (f32[2,512,256]{2,1,0:T(8,128)}, f32[2,512,256]{2,1,0:T(8,128)S(1)}, u32[]{:S(2)}) copy-start(f32[2,512,256]{2,1,0:T(8,128)S(1)} %collective-permute-done.6.cut_a) | copy-start | bytes 3145732
  111.1 1.3 %copy-start.2 = (f32[2,512,512]{2,1,0:T(8,128)}, f32[2,512,512]{2,1,0:T(8,128)S(1)}, u32[]{:S(2)}) copy-start(f32[2,512,512]{2,1,0:T(8,128)S(1)} %collective-permute-done.9.tri_in) | copy-start | bytes 6291460
  117.0 10.9 %collective-permute-start.10 = (f32[512,640]{1,0:T(8,128)}, f32[512,640]{1,0:T(8,128)S(1)}, u32[]{:S(2)}, u32[]{:S(2)}) collective-permute-start(f32[512,640]{1,0:T(8,128)} %get-tuple-element.18), channel_id=1, source_target_pairs={{0,1},{1,0},{2,3},{3,2},{4,5},{5,4},{6,7},{7,6},{8,9},{9,8},{10,11... | collective-permute-start | bytes 3932168 | tf_op jit(solution)/shard_map/ppermute | solution.py:259

commit v2 on v1

v2 whole, which is shorter than its diff:
```python
import jax
import jax.numpy as jnp
from jax import lax
from jax.experimental import pallas as pl
from jax.experimental.pallas import tpu as pltpu
from jax.sharding import PartitionSpec as P

AXES = ("cohort", "variant")
TILE = 512
HALF = 256
WIDTH = 640
F32 = jnp.float32
VMEM = 24 * 1024 * 1024


def route(blocks, rule):
    pairs = []
    for k in range(blocks // 2):
        for par in range(2):
            for lo in range(2):
                for core in range(2):
                    to = rule(k, par, lo, core)
                    if to is not None and 0 <= to[0] < blocks // 2:
                        source = (2 * k + par) * 4 + lo * 2 + core
                        pairs.append((source, (2 * to[0] + to[1]) * 4 + to[2] * 2 + to[3]))
    return pairs


def is_a(par, core):
    return core == par


def is_outer(par, lo):
    return lo == par


def to_mate(k, par, lo, core):
    if is_a(par, core):
        return (k, par, lo, 1 - core)
    return (k, 1 - par, lo, core)


def to_next(k, par, lo, core):
    return (k - 1 if core == 0 else k + 1, par, lo, core)


def to_chip(k, par, lo, core):
    return (k, par, 1 - lo, core) if is_a(par, core) else None


def to_across(k, par, lo, core):
    return None if is_a(par, core) else (k, par, 1 - lo, 1 - core)


def to_side(k, par, lo, core):
    return None if is_a(par, core) else (k, par, lo, 1 - core)


def to_far(k, par, lo, core):
    if is_a(par, core):
        return None
    return (k + 1 if core == 0 else k - 1, par, lo, 1 - core)


def to_mirror(k, par, lo, core):
    return (k, 1 - par, 1 - lo, 1 - core) if is_a(par, core) else None


def to_cut(k, par, lo, core):
    if is_a(par, core) and is_outer(par, lo):
        return (k + 1 if par == 0 else k - 1, par, lo, core)
    return None


def to_core(k, par, lo, core):
    return (k, par, lo, 1 - core) if is_a(par, core) else None


def dot_t(left, right):
    return lax.dot_general(left, right, (((1,), (1,)), ((), ())), preferred_element_type=F32)


def observed(data):
    total = data[0].astype(F32) + data[1].astype(F32) + data[2].astype(F32)
    return total.astype(jnp.bfloat16)


def pair_sums(left, left_obs, right, right_obs):
    cross = dot_t(left[0], right[2]) + dot_t(left[2], right[0])
    num = dot_t(left[1], right[1]) - 2.0 * cross
    den = dot_t(left[1], right_obs) + dot_t(left_obs, right[1])
    return num, den


def put_rows(first, second, values, swap):
    @pl.when(swap)
    def _():
        for i in range(2):
            first[i] = values[i][HALF:]
            second[i] = values[i][:HALF]

    @pl.when(jnp.logical_not(swap))
    def _():
        for i in range(2):
            first[i] = values[i][:HALF]
            second[i] = values[i][HALF:]


def put_tiles(tri, values, par, beyond):
    def put(parity, reach, first, second):
        @pl.when((par == parity) & (beyond == reach))
        def _():
            for i in range(2):
                tri[i, :HALF] = values[i][first]
                tri[i, HALF:] = values[i][second]

    low, high = slice(0, HALF), slice(HALF, TILE)
    put(0, 1, (high, low), (high, high))
    put(0, 0, (high, low), (low, low))
    put(1, 1, (low, high), (low, low))
    put(1, 0, (low, high), (high, high))


def fetch(source, target, sems, order=(1, 0, 2)):
    for plane in order:
        pltpu.make_async_copy(source.at[plane], target.at[plane], sems.at[plane]).start()


def arrived(source, target, sems, plane):
    pltpu.make_async_copy(source.at[plane], target.at[plane], sems.at[plane]).wait()


def first_kernel(role, own, mate, far, send_a, send_b, tri, left, right, left_sems, right_sems):
    par, lo, core, beyond = role[0], role[1], role[2], role[3]
    kind_a = core == par
    outer = lo == par

    @pl.when(kind_a & outer)
    def _():
        fetch(own, left, left_sems)
        fetch(mate, right, right_sems, (1, 2, 0))

    @pl.when(kind_a & jnp.logical_not(outer))
    def _():
        fetch(far, left, left_sems)
        fetch(mate, right, right_sems, (1, 2, 0))

    @pl.when(jnp.logical_not(kind_a))
    def _():
        fetch(far, left, left_sems)
        fetch(own, right, right_sems, (1, 2, 0))

    arrived(own, left, left_sems, 1)
    arrived(own, right, right_sems, 1)
    same = dot_t(left[1], right[1])
    arrived(own, left, left_sems, 0)
    arrived(own, right, right_sems, 2)
    cross = dot_t(left[0], right[2])
    arrived(own, left, left_sems, 2)
    arrived(own, right, right_sems, 0)
    cross = cross + dot_t(left[2], right[0])
    den = dot_t(left[1], observed(right)) + dot_t(observed(left), right[1])
    values = (same - 2.0 * cross, den)

    @pl.when(kind_a)
    def _():
        put_rows(send_a, send_b, values, outer == (par == 0))

    @pl.when(jnp.logical_not(kind_a))
    def _():
        put_tiles(tri, values, par, beyond)


def second_kernel(role, own, mate, far, keep_a, keep_b, tri, send_d, keep_d, own_v, mate_v, far_v, sems):
    par, lo, core, beyond = role[0], role[1], role[2], role[3]
    kind_a = core == par
    outer = lo == par

    def ready(source, target, which):
        for plane in (1, 0, 2):
            arrived(source, target, sems.at[which], plane)

    fetch(own, own_v, sems.at[0])

    @pl.when(kind_a)
    def _():
        fetch(far, far_v, sems.at[2])

    fetch(mate, mate_v, sems.at[1])
    ready(own, own_v, 0)
    own_obs = observed(own_v)

    @pl.when(kind_a)
    def _():
        ready(far, far_v, 2)
        far_obs = observed(far_v)
        put_tiles(tri, pair_sums(own_v, own_obs, far_v, far_obs), par, beyond)
        ready(mate, mate_v, 1)
        mate_obs = observed(mate_v)

        @pl.when(outer)
        def _():
            put_rows(keep_a, keep_b, pair_sums(far_v, far_obs, mate_v, mate_obs), par == 1)

        @pl.when(jnp.logical_not(outer))
        def _():
            put_rows(keep_a, keep_b, pair_sums(own_v, own_obs, mate_v, mate_obs), par == 0)

    @pl.when(jnp.logical_not(kind_a))
    def _():
        first = pair_sums(own_v, own_obs, own_v, own_obs)
        ready(mate, mate_v, 1)
        mate_obs = observed(mate_v)
        second = pair_sums(mate_v, mate_obs, mate_v, mate_obs)
        diag = (first[0] + second[0], first[1] + second[1])

        @pl.when(lo == 0)
        def _():
            for i in range(2):
                keep_d[i] = diag[i][:, :HALF]
                send_d[i] = diag[i][:, HALF:]

        @pl.when(lo == 1)
        def _():
            for i in range(2):
                send_d[i] = diag[i][:, :HALF]
                keep_d[i] = diag[i][:, HALF:]


def merge_kernel(role, held, kept, tri, tri_in, send, keep):
    par, lo, core = role[0], role[1], role[2]
    outer = lo == par
    row = lax.broadcasted_iota(jnp.int32, (HALF, HALF), 0)

    def near(source, target):
        first = jnp.where(par == 0, 0, HALF - role[5])
        free = (row >= first) & (row < first + role[5])
        for i in range(2):
            tile = (tri[i, :HALF] + tri_in[i, :HALF]).T
            other = (tri[i, HALF:] + tri_in[i, HALF:]).T

            @pl.when(par == 0)
            def _():
                target[i, :, HALF:] = jnp.where(free, tile, source[i, :, HALF:])
                target[i, :, :HALF] = jnp.where(free, other, source[i, :, :HALF])

            @pl.when(par == 1)
            def _():
                target[i, :, :HALF] = jnp.where(free, tile, source[i, :, :HALF])
                target[i, :, HALF:] = jnp.where(free, other, source[i, :, HALF:])

    def across(source, target):
        first = jnp.where(par == 0, HALF - role[6], 0)
        free = (row >= first) & (row < first + role[6])
        for i in range(2):
            tile = tri[i, :HALF] + tri_in[i, :HALF]
            other = tri[i, HALF:] + tri_in[i, HALF:]

            @pl.when(par == 0)
            def _():
                target[i, :, :HALF] = jnp.where(free, tile, source[i, :, :HALF])
                target[i, :, HALF:] = jnp.where(free, other, source[i, :, HALF:])

            @pl.when(par == 1)
            def _():
                target[i, :, HALF:] = jnp.where(free, tile, source[i, :, HALF:])
                target[i, :, :HALF] = jnp.where(free, other, source[i, :, :HALF])

    @pl.when((core == par) & outer)
    def _():
        near(held, send)
        across(kept, keep)

    @pl.when((core == par) & jnp.logical_not(outer))
    def _():
        across(held, send)
        near(kept, keep)


def ratio(num, den):
    return num / jnp.maximum(den, 1.0)


def ratio_kernel(role, full_a, full_b, mirror_a, mirror_b, cut_a, cut_b, diag, diag_in, send, keep):
    par, lo, core, beyond = role[0], role[1], role[2], role[4]
    kind_a = core == par
    outer = lo == par

    def ordered(first, second, i, swap):
        pair = (second[i], first[i]) if swap else (first[i], second[i])
        return jnp.concatenate(pair, axis=0)

    def behind(parity):
        flip = parity == 1
        num, den = [
            ordered(cut_a, cut_b, i, flip) + ordered(mirror_a, mirror_b, i, not flip).T
            for i in range(2)
        ]
        return ratio(num, den)

    def ahead(parity):
        flip = parity == 0
        num, den = [
            ordered(full_a, full_b, i, flip) + ordered(mirror_a, mirror_b, i, not flip).T
            for i in range(2)
        ]
        return ratio(num, den)

    def put_diag(target, start):
        target[:, start : start + HALF] = ratio(diag[0] + diag_in[0], diag[1] + diag_in[1])

    def put_tiles_at(target, start, parity, source, flip):
        near_x = HALF if parity == 0 else 0
        near_z = HALF - near_x
        both = near_z if flip else near_x
        first, second = [
            ratio(source[0, :, at : at + HALF], source[1, :, at : at + HALF]).T
            for at in (both, HALF - both)
        ]

        def place(x, z, value):
            row, col = (z, x) if flip else (x, z)
            target[row : row + HALF, start + col : start + col + HALF] = value

        zero = jnp.zeros((HALF, HALF), F32)
        place(near_x, near_z, first)
        place(HALF - near_x, HALF - near_z, zero)

        @pl.when(beyond == 1)
        def _():
            place(near_x, HALF - near_z, second)
            place(HALF - near_x, near_z, zero)

        @pl.when(beyond == 0)
        def _():
            place(HALF - near_x, near_z, second)
            place(near_x, HALF - near_z, zero)

    def when(parity, want_outer):
        return pl.when((par == parity) & kind_a & (outer == want_outer))

    @when(0, True)
    def _():
        value = behind(0)
        put_tiles_at(keep, 0, 0, cut_b, True)
        keep[:, 512:] = value[:, :128]
        send[:, :384] = value[:, 128:]
        put_diag(send, 384)

    @when(1, True)
    def _():
        value = behind(1)
        keep[:, :128] = value[:, 384:]
        put_tiles_at(keep, 128, 1, cut_b, True)
        put_diag(send, 0)
        send[:, 256:] = value[:, :384]

    @when(0, False)
    def _():
        value = ahead(0)
        put_diag(keep, 0)
        keep[:, 256:] = value[:, :384]
        send[:, :128] = value[:, 384:]
        put_tiles_at(send, 128, 0, full_b, False)

    @when(1, False)
    def _():
        value = ahead(1)
        put_tiles_at(send, 0, 1, full_b, False)
        send[:, 512:] = value[:, :128]
        keep[:, :384] = value[:, 128:]
        put_diag(keep, 384)


def place_kernel(role, row_cohort, col_cohort, keep, came, out):
    same = row_cohort[...] == col_cohort[...]

    @pl.when(role[2] == role[0])
    def _():
        out[...] = jnp.where(same, keep[...], 0.0)

    @pl.when(role[2] != role[0])
    def _():
        out[...] = jnp.where(same, came[...], 0.0)


def cohort_of(positions, cohort_ends):
    return jnp.sum((cohort_ends[None, :] <= positions[:, None]).astype(jnp.int32), axis=1)


def call(kernel, out_shapes, in_count, scratch=(), space=pltpu.VMEM):
    vmem = pl.BlockSpec(memory_space=pltpu.VMEM)
    return pl.pallas_call(
        kernel,
        out_shape=out_shapes,
        in_specs=[pl.BlockSpec(memory_space=pltpu.SMEM)] + [pl.BlockSpec(memory_space=space)] * in_count,
        out_specs=jax.tree.map(lambda _: vmem, out_shapes),
        scratch_shapes=list(scratch),
        compiler_params=pltpu.CompilerParams(vmem_limit_bytes=VMEM),
    )


def per_device(probs, cohort_sizes):
    blocks = lax.axis_size("cohort")
    block = lax.axis_index("cohort")
    quarter = lax.axis_index("variant")
    par, lo, core = block % 2, quarter // 2, quarter % 2
    kind_a = core == par
    outer = lo == par
    cohort_ends = jnp.cumsum(cohort_sizes)

    def cohorts(start):
        position = start * TILE + jnp.arange(TILE, dtype=jnp.int32)
        return jnp.where(position < 0, -1, cohort_of(position, cohort_ends))

    step = jnp.where(par == 0, 2, -2)
    own_ids, ahead_ids, back_ids = cohorts(block), cohorts(block + step), cohorts(block - step)
    even = par == 0

    def split(ids, low):
        low_half, high_half = ids[:HALF], ids[HALF:]
        return jnp.where(low, low_half, high_half), jnp.where(low, high_half, low_half)

    def reach(x_ids, z_ids):
        x_near, _ = split(x_ids, jnp.logical_not(even))
        z_near, z_far = split(z_ids, even)
        x_edge = jnp.where(even, x_ids[-1], x_ids[0])
        z_edge = jnp.where(even, z_ids[0], z_ids[-1])
        beyond = jnp.any(z_far == x_edge)
        return jnp.sum(z_near == x_edge), jnp.sum(x_near == z_edge), beyond

    z_count, x_count, beyond_ahead = reach(own_ids, ahead_ids)
    _, _, beyond_back = reach(back_ids, own_ids)
    role = jnp.stack(
        [
            par,
            lo,
            core,
            jnp.where(kind_a, beyond_ahead, beyond_back),
            jnp.where(outer, beyond_back, beyond_ahead),
            z_count,
            x_count,
        ]
    ).astype(jnp.int32)

    def move(value, rule):
        return lax.ppermute(value, AXES, route(blocks, rule))

    mate = move(probs, to_mate)
    far = move(probs, to_next)
    half = jax.ShapeDtypeStruct((2, TILE, HALF), F32)
    rows = jax.ShapeDtypeStruct((2, HALF, TILE), F32)
    block_of = pltpu.VMEM(probs.shape, probs.dtype)
    planes = pltpu.SemaphoreType.DMA((3,))
    send_a, held_b, send_t = call(
        first_kernel, (rows, rows, half), 3, (block_of, block_of, planes, planes), pltpu.HBM
    )(role, probs, mate, far)
    came_a = move(send_a, to_chip)
    tri_in = move(send_t, to_far)
    keep_a, kept_b, tri, send_d, keep_d = call(
        second_kernel,
        (rows, rows, half, half, half),
        3,
        (block_of, block_of, block_of, pltpu.SemaphoreType.DMA((3, 3))),
        pltpu.HBM,
    )(role, probs, mate, far)
    send_b, keep_b = call(merge_kernel, (rows, rows), 4)(role, held_b, kept_b, tri, tri_in)
    came_b = move(send_b, to_chip)
    full_a = keep_a + came_a
    mirror_a = move(full_a, to_mirror)
    cut_a = move(full_a, to_cut)
    send_d, keep_d, came_b = lax.optimization_barrier((send_d, keep_d, came_b))
    full_b = keep_b + came_b
    mirror_b = move(full_b, to_mirror)
    cut_b = move(full_b, to_cut)
    diag_in = move(send_d, to_across)
    diag = move(keep_d, to_side)
    wide = jax.ShapeDtypeStruct((TILE, WIDTH), F32)
    send, keep = call(ratio_kernel, (wide, wide), 8)(
        role, full_a, full_b, mirror_a, mirror_b, cut_a, cut_b, diag, diag_in
    )
    came = move(send, to_core)

    col_pos = (block - 2) * TILE + quarter * WIDTH + jnp.arange(WIDTH, dtype=jnp.int32)
    inside = (col_pos >= 0) & (col_pos < TILE * blocks)
    row_cohort = own_ids[:, None]
    col_cohort = jnp.where(inside, cohort_of(col_pos, cohort_ends), -1)[None, :]
    return call(place_kernel, wide, 4)(role, row_cohort, col_cohort, keep, came)


def solution(mesh):
    return jax.shard_map(
        per_device,
        mesh=mesh,
        in_specs=(P(None, "cohort", "variant"), P()),
        out_specs=P("cohort", "variant"),
        check_vma=False,
    )
```

time: 132 us -> 111 us (0.84)
  waiting for transfers between devices: 80.8 us -> 39.2 us
  starting transfers between devices: 25.6 us -> 40.4 us
  between operations: 0.28 us -> 6.69 us
  local copies, waits for them, and re-layouts: 1.59 us -> 5.86 us
  Pallas kernels: 18.7 us -> 14.9 us
    ppermute x11 -> x12, waiting for transfers between devices: 80.8 us -> 39.2 us  [move(): return lax.ppermute(value, AXES, route(blocks, rule))]
    ppermute x11 -> x12, starting transfers between devices: 25.6 us -> 40.4 us  [move(): return lax.ppermute(value, AXES, route(blocks, rule))]
    pallas_call x2 -> x4, Pallas kernels: 16.9 us -> 13.1 us  [the longest x1 6.51 us: per_device(): call(second_kernel, (rows, rows, half, half, half), 3, (block_of, block_o...]
    slice x0 -> x3, local copies, waits for them, and re-layouts: none -> 1.98 us  [the longest x2 1.32 us: reach(): x_edge = jnp.where(even, x_ids[-1], x_ids[0])]
    another operation x1 -> x2, local copies, waits for them, and re-layouts: 0.1 us -> 2.07 us  [the longest x1 1.32 us: per_device(): jnp.stack([par, lo, core, jnp.where(kind_a, beyond_ahead, beyond_back), j...]
    add x4 -> x5, other arithmetic: 2.35 us -> 0.43 us  [the longest x1 0.21 us: per_device(): full_a = keep_a + came_a]
    reduce_sum x0 -> x2, other arithmetic: none -> 1.33 us  [reach(): return (jnp.sum(z_near == x_edge), jnp.sum(x_near == z_edge), beyond)]
  transfers between devices with their start and end apart: 11 -> 12, of which waited for: 5 -> 5; matrix products, arithmetic and copies ran while one was open for 2% -> 6% of each run, Pallas kernels for 0% -> 6%
where the time goes in v2:
time: 111 us; the launch traced here: 110 us
  starting transfers between devices  40.4 us (36%)
  waiting for transfers between devices  39.2 us (35%)
  Pallas kernels  14.9 us (13%)
  between operations  6.69 us (6%)
  local copies, waits for them, and re-layouts  5.86 us (5%)
  other arithmetic  2.93 us (3%)
    ppermute x12, starting transfers between devices, move(): return lax.ppermute(value, AXES, route(blocks, rule))  40.4 us
    ppermute x12, waiting for transfers between devices, move(): return lax.ppermute(value, AXES, route(blocks, rule))  39.2 us
    pallas_call x1, Pallas kernels, per_device(): call(second_kernel, (rows, rows, half, half, half), 3, (block_of, block_o...  6.51 us
    pallas_call x1, Pallas kernels, per_device(): call(first_kernel, (rows, rows, half), 3, (block_of, block_of, planes, pl...  4.38 us
  transfers between devices with their start and end apart: 12, of which 5 were waited for; matrix products, arithmetic and copies ran while one was open for 6% of the time, Pallas kernels for 6%

profile of v2, /device:TPU:7, one launch (start us, length us, event | category | flops | bytes accessed | tf_op | source)
XLA Modules:
  0.0 110.0 jit_solution(2113687777978974068)
XLA Ops:
  0.0 2.9 %collective-permute-start = (bf16[3,512,768]{2,1,0:T(8,128)(2,1)}, bf16[3,512,768]{2,1,0:T(8,128)(2,1)S(1)}, u32[]{:S(2)}, u32[]{:S(2)}) collective-permute-start(bf16[3,512,768]{2,1,0:T(8,128)(2,1)} %own.3), channel_id=1, source_target_pairs={{0,1},{1,5},{2,3},{3,7},{4,0},{5,4},{6,2},{7,6},{8,9},{9,13},{10,1... | collective-permute-start | bytes 7077896 | tf_op jit(solution)/shard_map/ppermute | solution.py:447
  2.9 3.5 %collective-permute-start.1 = (bf16[3,512,768]{2,1,0:T(8,128)(2,1)}, bf16[3,512,768]{2,1,0:T(8,128)(2,1)}, u32[]{:S(2)}, u32[]{:S(2)}) collective-permute-start(bf16[3,512,768]{2,1,0:T(8,128)(2,1)} %own.3), channel_id=1, source_target_pairs={{1,9},{3,11},{5,13},{7,15},{8,0},{9,17},{10,2},{11,19},{12,4},{13,... | collective-permute-start | bytes 7077896 | tf_op jit(solution)/shard_map/ppermute | solution.py:447
  6.5 0.8 copy.6
  7.2 0.1 reduce-window.8
  7.3 0.1 reduce
  7.5 0.1 convert_reduce_fusion.1
  7.6 0.7 fusion.5
  9.6 0.7 fusion.4
  11.6 0.7 compare_reduce_fusion
  14.8 0.7 fusion.3
  16.7 0.7 fusion.1
  17.4 0.6 fusion.2
  18.0 1.3 %stack.39.role = s32[7]{0:T(128)S(1)} concatenate(s32[1]{0:T(128)} %bitcast, s32[1]{0:T(128)} %bitcast.1, s32[1]{0:T(128)} %bitcast.2, s32[1]{0:T(128)} %bitcast.8, s32[1]{0:T(128)} %bitcast.9, s32[1]{0:T(128)} %bitcast.10, s32[1]{0:T(128)} %bitcast.13), dimensions={0} | concatenate | bytes 56 | tf_op jit(solution)/shard_map/stack | solution.py:434
  19.3 9.7 %collective-permute-done.mate = bf16[3,512,768]{2,1,0:T(8,128)(2,1)S(1)} collective-permute-done((bf16[3,512,768]{2,1,0:T(8,128)(2,1)}, bf16[3,512,768]{2,1,0:T(8,128)(2,1)S(1)}, u32[]{:S(2)}, u32[]{:S(2)}) %collective-permute-start) | collective-permute-done | bytes 2359328 | tf_op jit(solution)/shard_map/ppermute | solution.py:447
  29.0 8.2 %collective-permute-done.1.far = bf16[3,512,768]{2,1,0:T(8,128)(2,1)} collective-permute-done((bf16[3,512,768]{2,1,0:T(8,128)(2,1)}, bf16[3,512,768]{2,1,0:T(8,128)(2,1)}, u32[]{:S(2)}, u32[]{:S(2)}) %collective-permute-start.1) | collective-permute-done | bytes 2359328 | tf_op jit(solution)/shard_map/ppermute | solution.py:447
  37.2 0.0 copy-start
  37.2 1.7 %copy-done = bf16[3,512,768]{2,1,0:T(8,128)(2,1)S(1)} copy-done((bf16[3,512,768]{2,1,0:T(8,128)(2,1)S(1)}, bf16[3,512,768]{2,1,0:T(8,128)(2,1)}, u32[]{:S(2)}) %copy-start) | copy-done | bytes 2359320
  38.9 4.4 %shard_map.29 = (f32[2,256,512]{2,1,0:T(8,128)S(1)}, f32[2,256,512]{2,1,0:T(8,128)S(1)}, f32[2,512,256]{2,1,0:T(8,128)S(1)}) custom-call(s32[7]{0:T(128)S(1)} %stack.39.role, bf16[3,512,768]{2,1,0:T(8,128)(2,1)S(1)} %copy-done, bf16[3,512,768]{2,1,0:T(8,128)(2,1)S(1)} %collective-permute-done.mate, bf16[3,512,768]{2,1,0:T(8,128)(2,1)} %collective-permute-done.1.far), custom_call_target="tpu_custom_call" | custom-call | tf_op jit(solution)/shard_map/pallas_call | solution.py:455
  43.2 3.6 %collective-permute-start.3 = (f32[2,512,256]{2,1,0:T(8,128)S(1)}, f32[2,512,256]{2,1,0:T(8,128)S(1)}, u32[]{:S(2)}, u32[]{:S(2)}) collective-permute-start(f32[2,512,256]{2,1,0:T(8,128)S(1)} %get-tuple-element.25), channel_id=1, source_target_pairs={{4,13},{6,15},{9,0},{11,2},{12,21},{14,23},{17,8},{19,10},{20,29},... | collective-permute-start | bytes 3145736 | tf_op jit(solution)/shard_map/ppermute | solution.py:447
  46.8 0.7 collective-permute-start.2
  47.6 6.5 %shard_map.28 = (f32[2,256,512]{2,1,0:T(8,128)S(1)}, f32[2,256,512]{2,1,0:T(8,128)S(1)}, f32[2,512,256]{2,1,0:T(8,128)S(1)}, f32[2,512,256]{2,1,0:T(8,128)S(1)}, f32[2,512,256]{2,1,0:T(8,128)S(1)}) custom-call(s32[7]{0:T(128)S(1)} %stack.39.role, bf16[3,512,768]{2,1,0:T(8,128)(2,1)S(1)} %copy-done, bf16[3,512,768]{2,1,0:T(8,128)(2,1)S(1)} %collective-permute-done.mate, ...), custom_call_target="tpu_custom_call" | custom-call | tf_op jit(solution)/shard_map/pallas_call | solution.py:460
  54.1 4.4 %collective-permute-done.3.tri_in = f32[2,512,256]{2,1,0:T(8,128)S(1)} collective-permute-done((f32[2,512,256]{2,1,0:T(8,128)S(1)}, f32[2,512,256]{2,1,0:T(8,128)S(1)}, u32[]{:S(2)}, u32[]{:S(2)}) %collective-permute-start.3) | collective-permute-done | bytes 1048608 | tf_op jit(solution)/shard_map/ppermute | solution.py:447
  58.5 0.6 shard_map.30
  59.1 0.7 collective-permute-start.4
  59.8 0.0 collective-permute-done.2
  59.8 0.2 add.98.full_a
  60.0 0.7 collective-permute-start.5
  60.8 0.7 collective-permute-start.7
  61.5 0.0 collective-permute-done.4
  61.5 0.2 add.99.full_b
  61.7 0.7 collective-permute-start.6
  62.5 0.7 collective-permute-start.8
  63.2 21.6 %collective-permute-start.10 = (f32[2,512,256]{2,1,0:T(8,128)S(1)}, f32[2,512,256]{2,1,0:T(8,128)S(1)}, u32[]{:S(2)}, u32[]{:S(2)}) collective-permute-start(f32[2,512,256]{2,1,0:T(8,128)S(1)} %get-tuple-element.32), channel_id=1, source_target_pairs={{1,2},{3,0},{4,7},{6,5},{9,10},{11,8},{12,15},{14,13},{17,18},{19,... | collective-permute-start | bytes 3145736 | tf_op jit(solution)/shard_map/ppermute | solution.py:447
  84.8 0.0 collective-permute-done.5.mirror_a
  84.8 3.2 %collective-permute-start.9 = (f32[2,512,256]{2,1,0:T(8,128)S(1)}, f32[2,512,256]{2,1,0:T(8,128)S(1)}, u32[]{:S(2)}, u32[]{:S(2)}) collective-permute-start(f32[2,512,256]{2,1,0:T(8,128)S(1)} %get-tuple-element.31), channel_id=1, source_target_pairs={{1,0},{3,2},{4,5},{6,7},{9,8},{11,10},{12,13},{14,15},{17,16},{19,... | collective-permute-start | bytes 3145736 | tf_op jit(solution)/shard_map/ppermute | solution.py:447
  88.0 0.0 collective-permute-done.7.cut_a
  88.0 0.0 collective-permute-done.6.mirror_b
  88.0 0.0 collective-permute-done.8.cut_b
  88.0 8.4 %collective-permute-done.10.diag_in = f32[2,512,256]{2,1,0:T(8,128)S(1)} collective-permute-done((f32[2,512,256]{2,1,0:T(8,128)S(1)}, f32[2,512,256]{2,1,0:T(8,128)S(1)}, u32[]{:S(2)}, u32[]{:S(2)}) %collective-permute-start.10) | collective-permute-done | bytes 1048608 | tf_op jit(solution)/shard_map/ppermute | solution.py:447
  96.4 0.0 collective-permute-done.9.diag
  96.4 1.6 %shard_map.31 = (f32[512,640]{1,0:T(8,128)}, f32[512,640]{1,0:T(8,128)S(1)}) custom-call(s32[7]{0:T(128)S(1)} %stack.39.role, f32[2,256,512]{2,1,0:T(8,128)S(1)} %add.98.full_a, f32[2,256,512]{2,1,0:T(8,128)S(1)} %add.99.full_b, f32[2,256,512]{2,1,0:T(8,128)S(1)} %collective-permute-done.5.mirror_a, f32[2,256,512]{2,1,0:T(8,128)S(1)} %collective-permute-done.6.mirror_b, ...), custom_call_target="tpu_custom_call" | custom-call | tf_op jit(solution)/shard_map/pallas_call | solution.py:479
  98.1 1.3 %collective-permute-start.11 = (f32[512,640]{1,0:T(8,128)}, f32[512,640]{1,0:T(8,128)S(1)}, u32[]{:S(2)}, u32[]{:S(2)}) collective-permute-start(f32[512,640]{1,0:T(8,128)} %get-tuple-element.34), channel_id=1, source_target_pairs={{0,1},{2,3},{5,4},{7,6},{8,9},{10,11},{13,12},{15,14},{16,17},{18,... | collective-permute-start | bytes 3932168 | tf_op jit(solution)/shard_map/ppermute | solution.py:447
  99.3 0.1 copy.7
  99.5 0.1 convert_reduce_fusion
  99.7 8.5 %collective-permute-done.11.came = f32[512,640]{1,0:T(8,128)S(1)} collective-permute-done((f32[512,640]{1,0:T(8,128)}, f32[512,640]{1,0:T(8,128)S(1)}, u32[]{:S(2)}, u32[]{:S(2)}) %collective-permute-start.11) | collective-permute-done | bytes 1310752 | tf_op jit(solution)/shard_map/ppermute | solution.py:447
  108.2 1.8 %shard_map.32 = f32[512,640]{1,0:T(8,128)} custom-call(s32[7]{0:T(128)S(1)} %stack.39.role, s32[512,1]{1,0:T(8,128)S(1)} %fusion.row_cohort, s32[1,640]{1,0:T(1,128)S(1)} %and_select_fusion.col_cohort, f32[512,640]{1,0:T(8,128)S(1)} %get-tuple-element.33.keep, f32[512,640]{1,0:T(8,128)S(1)} %collective-permute-done.11.came), custom_call_target="tpu_custom_call" | custom-call | tf_op jit(solution)/shard_map/pallas_call | solution.py:488
  (9 shorter events, 0.1 us)
Async XLA Ops:
  0.0 29.0 %collective-permute-start = (bf16[3,512,768]{2,1,0:T(8,128)(2,1)}, bf16[3,512,768]{2,1,0:T(8,128)(2,1)S(1)}, u32[]{:S(2)}, u32[]{:S(2)}) collective-permute-start(bf16[3,512,768]{2,1,0:T(8,128)(2,1)} %own.3), channel_id=1, source_target_pairs={{0,1},{1,5},{2,3},{3,7},{4,0},{5,4},{6,2},{7,6},{8,9},{9,13},{10,1... | collective-permute-start | bytes 7077896 | tf_op jit(solution)/shard_map/ppermute | solution.py:447
  2.9 34.3 %collective-permute-start.1 = (bf16[3,512,768]{2,1,0:T(8,128)(2,1)}, bf16[3,512,768]{2,1,0:T(8,128)(2,1)}, u32[]{:S(2)}, u32[]{:S(2)}) collective-permute-start(bf16[3,512,768]{2,1,0:T(8,128)(2,1)} %own.3), channel_id=1, source_target_pairs={{1,9},{3,11},{5,13},{7,15},{8,0},{9,17},{10,2},{11,19},{12,4},{13,... | collective-permute-start | bytes 7077896 | tf_op jit(solution)/shard_map/ppermute | solution.py:447
  37.2 1.7 %copy-start = (bf16[3,512,768]{2,1,0:T(8,128)(2,1)S(1)}, bf16[3,512,768]{2,1,0:T(8,128)(2,1)}, u32[]{:S(2)}) copy-start(bf16[3,512,768]{2,1,0:T(8,128)(2,1)} %own.3) | copy-start | bytes 7077892
  43.2 15.2 %collective-permute-start.3 = (f32[2,512,256]{2,1,0:T(8,128)S(1)}, f32[2,512,256]{2,1,0:T(8,128)S(1)}, u32[]{:S(2)}, u32[]{:S(2)}) collective-permute-start(f32[2,512,256]{2,1,0:T(8,128)S(1)} %get-tuple-element.25), channel_id=1, source_target_pairs={{4,13},{6,15},{9,0},{11,2},{12,21},{14,23},{17,8},{19,10},{20,29},... | collective-permute-start | bytes 3145736 | tf_op jit(solution)/shard_map/ppermute | solution.py:447
  46.8 13.0 %collective-permute-start.2 = (f32[2,256,512]{2,1,0:T(8,128)S(1)}, f32[2,256,512]{2,1,0:T(8,128)S(1)}, u32[]{:S(2)}, u32[]{:S(2)}) collective-permute-start(f32[2,256,512]{2,1,0:T(8,128)S(1)} %get-tuple-element.21), channel_id=1, source_target_pairs={{0,2},{2,0},{5,7},{7,5},{8,10},{10,8},{13,15},{15,13},{16,18},{18,... | collective-permute-start | bytes 3145736 | tf_op jit(solution)/shard_map/ppermute | solution.py:447
  59.1 2.4 %collective-permute-start.4 = (f32[2,256,512]{2,1,0:T(8,128)S(1)}, f32[2,256,512]{2,1,0:T(8,128)S(1)}, u32[]{:S(2)}, u32[]{:S(2)}) collective-permute-start(f32[2,256,512]{2,1,0:T(8,128)S(1)} %get-tuple-element.29), channel_id=1, source_target_pairs={{0,2},{2,0},{5,7},{7,5},{8,10},{10,8},{13,15},{15,13},{16,18},{18,... | collective-permute-start | bytes 3145736 | tf_op jit(solution)/shard_map/ppermute | solution.py:447
  60.0 24.8 %collective-permute-start.5 = (f32[2,256,512]{2,1,0:T(8,128)S(1)}, f32[2,256,512]{2,1,0:T(8,128)S(1)}, u32[]{:S(2)}, u32[]{:S(2)}) collective-permute-start(f32[2,256,512]{2,1,0:T(8,128)S(1)} %add.98.full_a), channel_id=1, source_target_pairs={{0,7},{2,5},{5,2},{7,0},{8,15},{10,13},{13,10},{15,8},{16,23},{18,... | collective-permute-start | bytes 3145736 | tf_op jit(solution)/shard_map/ppermute | solution.py:447
  60.8 27.2 %collective-permute-start.7 = (f32[2,256,512]{2,1,0:T(8,128)S(1)}, f32[2,256,512]{2,1,0:T(8,128)S(1)}, u32[]{:S(2)}, u32[]{:S(2)}) collective-permute-start(f32[2,256,512]{2,1,0:T(8,128)S(1)} %add.98.full_a), channel_id=1, source_target_pairs={{0,8},{8,16},{15,7},{16,24},{23,15},{24,32},{31,23},{32,40},{39,31... | collective-permute-start | bytes 3145736 | tf_op jit(solution)/shard_map/ppermute | solution.py:447
  61.7 26.3 %collective-permute-start.6 = (f32[2,256,512]{2,1,0:T(8,128)S(1)}, f32[2,256,512]{2,1,0:T(8,128)S(1)}, u32[]{:S(2)}, u32[]{:S(2)}) collective-permute-start(f32[2,256,512]{2,1,0:T(8,128)S(1)} %add.99.full_b), channel_id=1, source_target_pairs={{0,7},{2,5},{5,2},{7,0},{8,15},{10,13},{13,10},{15,8},{16,23},{18,... | collective-permute-start | bytes 3145736 | tf_op jit(solution)/shard_map/ppermute | solution.py:447
  62.5 25.6 %collective-permute-start.8 = (f32[2,256,512]{2,1,0:T(8,128)S(1)}, f32[2,256,512]{2,1,0:T(8,128)S(1)}, u32[]{:S(2)}, u32[]{:S(2)}) collective-permute-start(f32[2,256,512]{2,1,0:T(8,128)S(1)} %add.99.full_b), channel_id=1, source_target_pairs={{0,8},{8,16},{15,7},{16,24},{23,15},{24,32},{31,23},{32,40},{39,31... | collective-permute-start | bytes 3145736 | tf_op jit(solution)/shard_map/ppermute | solution.py:447
  63.2 33.2 %collective-permute-start.10 = (f32[2,512,256]{2,1,0:T(8,128)S(1)}, f32[2,512,256]{2,1,0:T(8,128)S(1)}, u32[]{:S(2)}, u32[]{:S(2)}) collective-permute-start(f32[2,512,256]{2,1,0:T(8,128)S(1)} %get-tuple-element.32), channel_id=1, source_target_pairs={{1,2},{3,0},{4,7},{6,5},{9,10},{11,8},{12,15},{14,13},{17,18},{19,... | collective-permute-start | bytes 3145736 | tf_op jit(solution)/shard_map/ppermute | solution.py:447
  84.8 11.7 %collective-permute-start.9 = (f32[2,512,256]{2,1,0:T(8,128)S(1)}, f32[2,512,256]{2,1,0:T(8,128)S(1)}, u32[]{:S(2)}, u32[]{:S(2)}) collective-permute-start(f32[2,512,256]{2,1,0:T(8,128)S(1)} %get-tuple-element.31), channel_id=1, source_target_pairs={{1,0},{3,2},{4,5},{6,7},{9,8},{11,10},{12,13},{14,15},{17,16},{19,... | collective-permute-start | bytes 3145736 | tf_op jit(solution)/shard_map/ppermute | solution.py:447
  98.1 10.2 %collective-permute-start.11 = (f32[512,640]{1,0:T(8,128)}, f32[512,640]{1,0:T(8,128)S(1)}, u32[]{:S(2)}, u32[]{:S(2)}) collective-permute-start(f32[512,640]{1,0:T(8,128)} %get-tuple-element.34), channel_id=1, source_target_pairs={{0,1},{2,3},{5,4},{7,6},{8,9},{10,11},{13,12},{15,14},{16,17},{18,... | collective-permute-start | bytes 3932168 | tf_op jit(solution)/shard_map/ppermute | solution.py:447

commit v3 on v2

--- a/solution.py
+++ b/solution.py
@@ -106,19 +106,21 @@
             second[i] = values[i][HALF:]
 
 
-def put_tiles(tri, values, par, beyond):
-    def put(parity, reach, first, second):
-        @pl.when((par == parity) & (beyond == reach))
-        def _():
-            for i in range(2):
-                tri[i, :HALF] = values[i][first]
-                tri[i, HALF:] = values[i][second]
-
-    low, high = slice(0, HALF), slice(HALF, TILE)
-    put(0, 1, (high, low), (high, high))
-    put(0, 0, (high, low), (low, low))
-    put(1, 1, (low, high), (low, low))
-    put(1, 0, (low, high), (high, high))
+def put_tiles(tri, left, right, par, beyond):
+    near_left = jnp.where(par == 0, HALF, 0)
+    near_right = HALF - near_left
+    other_left = jnp.where(beyond == 1, near_left, near_right)
+    other_right = jnp.where(beyond == 1, near_left, near_right)
+
+    def rows(data, start):
+        at = pl.ds(pl.multiple_of(start, HALF), HALF)
+        return [data[plane, at, :] for plane in range(3)]
+
+    for tile, (l, r) in enumerate(((near_left, near_right), (other_left, other_right))):
+        left_rows, right_rows = rows(left, l), rows(right, r)
+        num, den = pair_sums(left_rows, observed(left_rows), right_rows, observed(right_rows))
+        tri[0, tile * HALF : (tile + 1) * HALF] = num
+        tri[1, tile * HALF : (tile + 1) * HALF] = den
 
 
 def fetch(source, target, sems, order=(1, 0, 2)):
@@ -130,88 +132,70 @@
     pltpu.make_async_copy(source.at[plane], target.at[plane], sems.at[plane]).wait()
 
 
-def first_kernel(role, own, mate, far, send_a, send_b, tri, left, right, left_sems, right_sems):
-    par, lo, core, beyond = role[0], role[1], role[2], role[3]
+def stage_kernel(role, own, out, out_obs):
+    out[...] = own[...]
+    out_obs[...] = observed(own)
+
+
+def tiles_kernel(role, own, far, tri, far_v, sems):
+    par, core, beyond = role[0], role[2], role[3]
+
+    @pl.when(core != par)
+    def _():
+        fetch(far, far_v, sems)
+        for plane in range(3):
+            arrived(far, far_v, sems, plane)
+        put_tiles(tri, far_v, own, par, beyond)
+
+
+def first_kernel(role, own, own_obs, mate, far, after, send_a, send_b, far_v, sems):
+    par, lo, core = role[0], role[1], role[2]
     kind_a = core == par
     outer = lo == par
 
     @pl.when(kind_a & outer)
     def _():
-        fetch(own, left, left_sems)
-        fetch(mate, right, right_sems, (1, 2, 0))
+        put_rows(send_a, send_b, pair_sums(own, own_obs[...], mate, observed(mate)), par == 0)
 
     @pl.when(kind_a & jnp.logical_not(outer))
     def _():
-        fetch(far, left, left_sems)
-        fetch(mate, right, right_sems, (1, 2, 0))
-
-    @pl.when(jnp.logical_not(kind_a))
-    def _():
-        fetch(far, left, left_sems)
-        fetch(own, right, right_sems, (1, 2, 0))
-
-    arrived(own, left, left_sems, 1)
-    arrived(own, right, right_sems, 1)
-    same = dot_t(left[1], right[1])
-    arrived(own, left, left_sems, 0)
-    arrived(own, right, right_sems, 2)
-    cross = dot_t(left[0], right[2])
-    arrived(own, left, left_sems, 2)
-    arrived(own, right, right_sems, 0)
-    cross = cross + dot_t(left[2], right[0])
-    den = dot_t(left[1], observed(right)) + dot_t(observed(left), right[1])
-    values = (same - 2.0 * cross, den)
-
-    @pl.when(kind_a)
-    def _():
-        put_rows(send_a, send_b, values, outer == (par == 0))
-
-    @pl.when(jnp.logical_not(kind_a))
-    def _():
-        put_tiles(tri, values, par, beyond)
-
-
-def second_kernel(role, own, mate, far, keep_a, keep_b, tri, send_d, keep_d, own_v, mate_v, far_v, sems):
+        fetch(far, far_v, sems)
+        mate_obs = observed(mate)
+        arrived(far, far_v, sems, 1)
+        same = dot_t(far_v[1], mate[1])
+        den = dot_t(far_v[1], mate_obs)
+        arrived(far, far_v, sems, 0)
+        cross = dot_t(far_v[0], mate[2])
+        arrived(far, far_v, sems, 2)
+        cross = cross + dot_t(far_v[2], mate[0])
+        den = den + dot_t(observed(far_v), mate[1])
+        put_rows(send_a, send_b, (same - 2.0 * cross, den), par == 1)
+
+
+def second_kernel(role, own, own_obs, mate, far, keep_a, keep_b, tri, send_d, keep_d, far_v, sems):
     par, lo, core, beyond = role[0], role[1], role[2], role[3]
-    kind_a = core == par
     outer = lo == par
 
-    def ready(source, target, which):
-        for plane in (1, 0, 2):
-            arrived(source, target, sems.at[which], plane)
-
-    fetch(own, own_v, sems.at[0])
-
-    @pl.when(kind_a)
-    def _():
-        fetch(far, far_v, sems.at[2])
-
-    fetch(mate, mate_v, sems.at[1])
-    ready(own, own_v, 0)
-    own_obs = observed(own_v)
-
-    @pl.when(kind_a)
-    def _():
-        ready(far, far_v, 2)
-        far_obs = observed(far_v)
-        put_tiles(tri, pair_sums(own_v, own_obs, far_v, far_obs), par, beyond)
-        ready(mate, mate_v, 1)
-        mate_obs = observed(mate_v)
+    @pl.when(core == par)
+    def _():
+        fetch(far, far_v, sems)
+        for plane in range(3):
+            arrived(far, far_v, sems, plane)
+        put_tiles(tri, own, far_v, par, beyond)
 
         @pl.when(outer)
         def _():
-            put_rows(keep_a, keep_b, pair_sums(far_v, far_obs, mate_v, mate_obs), par == 1)
+            put_rows(keep_a, keep_b, pair_sums(far_v, observed(far_v), mate, observed(mate)), par == 1)
 
         @pl.when(jnp.logical_not(outer))
         def _():
-            put_rows(keep_a, keep_b, pair_sums(own_v, own_obs, mate_v, mate_obs), par == 0)
-
-    @pl.when(jnp.logical_not(kind_a))
-    def _():
-        first = pair_sums(own_v, own_obs, own_v, own_obs)
-        ready(mate, mate_v, 1)
-        mate_obs = observed(mate_v)
-        second = pair_sums(mate_v, mate_obs, mate_v, mate_obs)
+            put_rows(keep_a, keep_b, pair_sums(own, own_obs[...], mate, observed(mate)), par == 0)
+
+    @pl.when(core != par)
+    def _():
+        first = pair_sums(own, own_obs[...], own, own_obs[...])
+        mate_obs = observed(mate)
+        second = pair_sums(mate, mate_obs, mate, mate_obs)
         diag = (first[0] + second[0], first[1] + second[1])
 
         @pl.when(lo == 0)
@@ -281,7 +265,7 @@
     return num / jnp.maximum(den, 1.0)
 
 
-def ratio_kernel(role, full_a, full_b, mirror_a, mirror_b, cut_a, cut_b, diag, diag_in, send, keep):
+def ratio_kernel(role, diag_in, diag, cut_a, cut_b, mirror_a, mirror_b, full_a, full_b, send, keep):
     par, lo, core, beyond = role[0], role[1], role[2], role[4]
     kind_a = core == par
     outer = lo == par
@@ -388,12 +372,12 @@
     return jnp.sum((cohort_ends[None, :] <= positions[:, None]).astype(jnp.int32), axis=1)
 
 
-def call(kernel, out_shapes, in_count, scratch=(), space=pltpu.VMEM):
+def call(kernel, out_shapes, spaces, scratch=()):
     vmem = pl.BlockSpec(memory_space=pltpu.VMEM)
     return pl.pallas_call(
         kernel,
         out_shape=out_shapes,
-        in_specs=[pl.BlockSpec(memory_space=pltpu.SMEM)] + [pl.BlockSpec(memory_space=space)] * in_count,
+        in_specs=[pl.BlockSpec(memory_space=pltpu.SMEM)] + [pl.BlockSpec(memory_space=space) for space in spaces],
         out_specs=jax.tree.map(lambda _: vmem, out_shapes),
         scratch_shapes=list(scratch),
         compiler_params=pltpu.CompilerParams(vmem_limit_bytes=VMEM),
@@ -446,38 +430,43 @@
     def move(value, rule):
         return lax.ppermute(value, AXES, route(blocks, rule))
 
+    far = move(probs, to_next)
     mate = move(probs, to_mate)
-    far = move(probs, to_next)
     half = jax.ShapeDtypeStruct((2, TILE, HALF), F32)
     rows = jax.ShapeDtypeStruct((2, HALF, TILE), F32)
     block_of = pltpu.VMEM(probs.shape, probs.dtype)
     planes = pltpu.SemaphoreType.DMA((3,))
-    send_a, held_b, send_t = call(
-        first_kernel, (rows, rows, half), 3, (block_of, block_of, planes, planes), pltpu.HBM
-    )(role, probs, mate, far)
+    obs = jax.ShapeDtypeStruct(probs.shape[1:], probs.dtype)
+    vmem = pltpu.VMEM
+    own, own_obs = call(stage_kernel, (jax.ShapeDtypeStruct(probs.shape, probs.dtype), obs), [vmem])(
+        role, probs
+    )
+    send_t = call(tiles_kernel, half, (vmem, pl.ANY), (block_of, planes))(role, own, far)
+    send_a, held_b = call(
+        first_kernel, (rows, rows), (vmem, vmem, vmem, pl.ANY, pl.ANY), (block_of, planes)
+    )(role, own, own_obs, mate, far, send_t)
+    tri_in = move(send_t, to_far)
     came_a = move(send_a, to_chip)
-    tri_in = move(send_t, to_far)
     keep_a, kept_b, tri, send_d, keep_d = call(
         second_kernel,
         (rows, rows, half, half, half),
-        3,
-        (block_of, block_of, block_of, pltpu.SemaphoreType.DMA((3, 3))),
-        pltpu.HBM,
-    )(role, probs, mate, far)
-    send_b, keep_b = call(merge_kernel, (rows, rows), 4)(role, held_b, kept_b, tri, tri_in)
+        (vmem, vmem, vmem, pl.ANY),
+        (block_of, planes),
+    )(role, own, own_obs, mate, far)
+    send_b, keep_b = call(merge_kernel, (rows, rows), [pltpu.VMEM] * 4)(role, held_b, kept_b, tri, tri_in)
     came_b = move(send_b, to_chip)
     full_a = keep_a + came_a
     mirror_a = move(full_a, to_mirror)
     cut_a = move(full_a, to_cut)
     send_d, keep_d, came_b = lax.optimization_barrier((send_d, keep_d, came_b))
+    diag_in = move(send_d, to_across)
     full_b = keep_b + came_b
+    cut_b = move(full_b, to_cut)
     mirror_b = move(full_b, to_mirror)
-    cut_b = move(full_b, to_cut)
-    diag_in = move(send_d, to_across)
     diag = move(keep_d, to_side)
     wide = jax.ShapeDtypeStruct((TILE, WIDTH), F32)
-    send, keep = call(ratio_kernel, (wide, wide), 8)(
-        role, full_a, full_b, mirror_a, mirror_b, cut_a, cut_b, diag, diag_in
+    send, keep = call(ratio_kernel, (wide, wide), [pltpu.VMEM] * 8)(
+        role, diag_in, diag, cut_a, cut_b, mirror_a, mirror_b, full_a, full_b
     )
     came = move(send, to_core)
 
@@ -485,7 +474,7 @@
     inside = (col_pos >= 0) & (col_pos < TILE * blocks)
     row_cohort = own_ids[:, None]
     col_cohort = jnp.where(inside, cohort_of(col_pos, cohort_ends), -1)[None, :]
-    return call(place_kernel, wide, 4)(role, row_cohort, col_cohort, keep, came)
+    return call(place_kernel, wide, [pltpu.VMEM] * 4)(role, row_cohort, col_cohort, keep, came)
 
 
 def solution(mesh):

time: 111 us -> 106 us (0.955)
  waiting for transfers between devices: 39.2 us -> 32.3 us
  starting transfers between devices: 40.4 us -> 41.8 us
    ppermute x12, waiting for transfers between devices: 39.2 us -> 32.3 us  [move(): return lax.ppermute(value, AXES, route(blocks, rule))]
    ppermute x12, starting transfers between devices: 40.4 us -> 41.8 us  [move(): return lax.ppermute(value, AXES, route(blocks, rule))]
    pallas_call x5 -> x7, Pallas kernels: 14.9 us -> 15.2 us  [the longest x1 6.31 us: per_device(): call(second_kernel, (rows, rows, half, half, half), (vmem, vmem, vmem, pl...]
  transfers between devices with their start and end apart: 12 -> 12, of which waited for: 5 -> 4; matrix products, arithmetic and copies ran while one was open for 6% -> 7% of each run, Pallas kernels for 6% -> 11%
where the time goes in v3:
time: 106 us; the launch traced here: 105 us
  starting transfers between devices  41.8 us (39%)
  waiting for transfers between devices  32.3 us (30%)
  Pallas kernels  15.2 us (14%)
  between operations  6.68 us (6%)
  local copies, waits for them, and re-layouts  5.86 us (6%)
  other arithmetic  2.93 us (3%)
    ppermute x12, starting transfers between devices, move(): return lax.ppermute(value, AXES, route(blocks, rule))  41.8 us
    ppermute x12, waiting for transfers between devices, move(): return lax.ppermute(value, AXES, route(blocks, rule))  32.3 us
    pallas_call x1, Pallas kernels, per_device(): call(second_kernel, (rows, rows, half, half, half), (vmem, vmem, vmem, pl...  6.31 us
    pallas_call x1, Pallas kernels, per_device(): call(tiles_kernel, half, (vmem, pl.ANY), (block_of, planes))(role, own, far)  2.21 us
  transfers between devices with their start and end apart: 12, of which 4 were waited for; matrix products, arithmetic and copies ran while one was open for 7% of the time, Pallas kernels for 11%

profile of v3, /device:TPU:7, one launch (start us, length us, event | category | flops | bytes accessed | tf_op | source)
XLA Modules:
  0.0 104.8 jit_solution(11501013222724668173)
XLA Ops:
  0.0 3.5 %collective-permute-start.1 = (bf16[3,512,768]{2,1,0:T(8,128)(2,1)}, bf16[3,512,768]{2,1,0:T(8,128)(2,1)S(1)}, u32[]{:S(2)}, u32[]{:S(2)}) collective-permute-start(bf16[3,512,768]{2,1,0:T(8,128)(2,1)} %own.1), channel_id=1, source_target_pairs={{1,9},{3,11},{5,13},{7,15},{8,0},{9,17},{10,2},{11,19},{12,4},{13,... | collective-permute-start | bytes 7077896 | tf_op jit(solution)/shard_map/ppermute | solution.py:431
  3.5 3.0 %collective-permute-start = (bf16[3,512,768]{2,1,0:T(8,128)(2,1)}, bf16[3,512,768]{2,1,0:T(8,128)(2,1)}, u32[]{:S(2)}, u32[]{:S(2)}) collective-permute-start(bf16[3,512,768]{2,1,0:T(8,128)(2,1)} %own.1), channel_id=1, source_target_pairs={{0,1},{1,5},{2,3},{3,7},{4,0},{5,4},{6,2},{7,6},{8,9},{9,13},{10,1... | collective-permute-start | bytes 7077896 | tf_op jit(solution)/shard_map/ppermute | solution.py:431
  6.5 0.8 copy.6
  7.3 0.1 reduce-window.8
  7.4 0.1 reduce
  7.5 0.1 convert_reduce_fusion.1
  7.7 0.7 fusion.5
  9.7 0.7 fusion.4
  11.6 0.7 compare_reduce_fusion
  14.8 0.7 fusion.3
  16.7 0.7 fusion.1
  17.5 0.6 fusion.2
  18.1 1.3 %stack.39.role = s32[7]{0:T(128)S(1)} concatenate(s32[1]{0:T(128)} %bitcast, s32[1]{0:T(128)} %bitcast.1, s32[1]{0:T(128)} %bitcast.2, s32[1]{0:T(128)} %bitcast.8, s32[1]{0:T(128)} %bitcast.9, s32[1]{0:T(128)} %bitcast.10, s32[1]{0:T(128)} %bitcast.13), dimensions={0} | concatenate | bytes 56 | tf_op jit(solution)/shard_map/stack | solution.py:418
  19.4 0.0 copy-start
  19.4 1.7 %copy-done = bf16[3,512,768]{2,1,0:T(8,128)(2,1)S(1)} copy-done((bf16[3,512,768]{2,1,0:T(8,128)(2,1)S(1)}, bf16[3,512,768]{2,1,0:T(8,128)(2,1)}, u32[]{:S(2)}) %copy-start) | copy-done | bytes 2359320
  21.1 1.0 shard_map.28
  22.0 12.5 %collective-permute-done.1.far = bf16[3,512,768]{2,1,0:T(8,128)(2,1)S(1)} collective-permute-done((bf16[3,512,768]{2,1,0:T(8,128)(2,1)}, bf16[3,512,768]{2,1,0:T(8,128)(2,1)S(1)}, u32[]{:S(2)}, u32[]{:S(2)}) %collective-permute-start.1) | collective-permute-done | bytes 2359328 | tf_op jit(solution)/shard_map/ppermute | solution.py:431
  34.6 2.2 %shard_map.30.after = f32[2,512,256]{2,1,0:T(8,128)S(1)} custom-call(s32[7]{0:T(128)S(1)} %stack.39.role, bf16[3,512,768]{2,1,0:T(8,128)(2,1)S(1)} %get-tuple-element.21.own, bf16[3,512,768]{2,1,0:T(8,128)(2,1)S(1)} %collective-permute-done.1.far), custom_call_target="tpu_custom_call" | custom-call | tf_op jit(solution)/shard_map/pallas_call | solution.py:444
  36.8 5.2 %collective-permute-start.2 = (f32[2,512,256]{2,1,0:T(8,128)S(1)}, f32[2,512,256]{2,1,0:T(8,128)S(1)}, u32[]{:S(2)}, u32[]{:S(2)}) collective-permute-start(f32[2,512,256]{2,1,0:T(8,128)S(1)} %shard_map.30.after), channel_id=1, source_target_pairs={{4,13},{6,15},{9,0},{11,2},{12,21},{14,23},{17,8},{19,10},{20,29},... | collective-permute-start | bytes 3145736 | tf_op jit(solution)/shard_map/ppermute | solution.py:431
  42.0 0.0 collective-permute-done.mate
  42.0 1.7 %shard_map.31 = (f32[2,256,512]{2,1,0:T(8,128)S(1)}, f32[2,256,512]{2,1,0:T(8,128)S(1)}) custom-call(s32[7]{0:T(128)S(1)} %stack.39.role, bf16[3,512,768]{2,1,0:T(8,128)(2,1)S(1)} %get-tuple-element.21.own, bf16[512,768]{1,0:T(8,128)(2,1)S(1)} %get-tuple-element.22.own_obs, bf16[3,512,768]{2,1,0:T(8,128)(2,1)} %collective-permute-done.mate, ...), custom_call_target="tpu_custom_call" | custom-call | tf_op jit(solution)/shard_map/pallas_call | solution.py:445
  43.7 0.7 collective-permute-start.6
  44.5 6.3 %shard_map.29 = (f32[2,256,512]{2,1,0:T(8,128)S(1)}, f32[2,256,512]{2,1,0:T(8,128)S(1)}, f32[2,512,256]{2,1,0:T(8,128)S(1)}, f32[2,512,256]{2,1,0:T(8,128)S(1)}, f32[2,512,256]{2,1,0:T(8,128)S(1)}) custom-call(s32[7]{0:T(128)S(1)} %stack.39.role, bf16[3,512,768]{2,1,0:T(8,128)(2,1)S(1)} %get-tuple-element.21.own, ...), custom_call_target="tpu_custom_call" | custom-call | tf_op jit(solution)/shard_map/pallas_call | solution.py:450
  50.8 2.9 %collective-permute-done.2.tri_in = f32[2,512,256]{2,1,0:T(8,128)S(1)} collective-permute-done((f32[2,512,256]{2,1,0:T(8,128)S(1)}, f32[2,512,256]{2,1,0:T(8,128)S(1)}, u32[]{:S(2)}, u32[]{:S(2)}) %collective-permute-start.2) | collective-permute-done | bytes 1048608 | tf_op jit(solution)/shard_map/ppermute | solution.py:431
  53.7 0.6 shard_map.32
  54.2 0.7 collective-permute-start.3
  55.0 0.0 collective-permute-done.6
  55.0 0.2 add.98.full_a
  55.2 0.7 collective-permute-start.7
  55.9 0.7 collective-permute-start.9
  56.7 0.0 collective-permute-done.3
  56.7 0.2 add.99.full_b
  56.9 0.7 collective-permute-start.10
  57.6 0.7 collective-permute-start.8
  58.4 21.7 %collective-permute-start.4 = (f32[2,512,256]{2,1,0:T(8,128)S(1)}, f32[2,512,256]{2,1,0:T(8,128)S(1)}, u32[]{:S(2)}, u32[]{:S(2)}) collective-permute-start(f32[2,512,256]{2,1,0:T(8,128)S(1)} %get-tuple-element.29), channel_id=1, source_target_pairs={{1,2},{3,0},{4,7},{6,5},{9,10},{11,8},{12,15},{14,13},{17,18},{19,... | collective-permute-start | bytes 3145736 | tf_op jit(solution)/shard_map/ppermute | solution.py:431
  80.0 0.0 collective-permute-done.7.cut_a
  80.1 2.7 %collective-permute-start.5 = (f32[2,512,256]{2,1,0:T(8,128)S(1)}, f32[2,512,256]{2,1,0:T(8,128)S(1)}, u32[]{:S(2)}, u32[]{:S(2)}) collective-permute-start(f32[2,512,256]{2,1,0:T(8,128)S(1)} %get-tuple-element.30), channel_id=1, source_target_pairs={{1,0},{3,2},{4,5},{6,7},{9,8},{11,10},{12,13},{14,15},{17,16},{19,... | collective-permute-start | bytes 3145736 | tf_op jit(solution)/shard_map/ppermute | solution.py:431
  82.8 0.0 collective-permute-done.9.mirror_a
  82.8 0.0 collective-permute-done.10.mirror_b
  82.8 0.0 collective-permute-done.8.cut_b
  82.8 8.9 %collective-permute-done.4.diag_in = f32[2,512,256]{2,1,0:T(8,128)S(1)} collective-permute-done((f32[2,512,256]{2,1,0:T(8,128)S(1)}, f32[2,512,256]{2,1,0:T(8,128)S(1)}, u32[]{:S(2)}, u32[]{:S(2)}) %collective-permute-start.4) | collective-permute-done | bytes 1048608 | tf_op jit(solution)/shard_map/ppermute | solution.py:431
  91.7 0.0 collective-permute-done.5.diag
  91.7 1.6 %shard_map.33 = (f32[512,640]{1,0:T(8,128)}, f32[512,640]{1,0:T(8,128)S(1)}) custom-call(s32[7]{0:T(128)S(1)} %stack.39.role, f32[2,512,256]{2,1,0:T(8,128)S(1)} %collective-permute-done.4.diag_in, f32[2,512,256]{2,1,0:T(8,128)S(1)} %collective-permute-done.5.diag, f32[2,256,512]{2,1,0:T(8,128)S(1)} %collective-permute-done.7.cut_a, ...), custom_call_target="tpu_custom_call" | custom-call | tf_op jit(solution)/shard_map/pallas_call | solution.py:468
  93.3 1.3 %collective-permute-start.11 = (f32[512,640]{1,0:T(8,128)}, f32[512,640]{1,0:T(8,128)S(1)}, u32[]{:S(2)}, u32[]{:S(2)}) collective-permute-start(f32[512,640]{1,0:T(8,128)} %get-tuple-element.36), channel_id=1, source_target_pairs={{0,1},{2,3},{5,4},{7,6},{8,9},{10,11},{13,12},{15,14},{16,17},{18,... | collective-permute-start | bytes 3932168 | tf_op jit(solution)/shard_map/ppermute | solution.py:431
  94.6 0.1 copy.7
  94.8 0.1 convert_reduce_fusion
  95.0 8.1 %collective-permute-done.11.came = f32[512,640]{1,0:T(8,128)S(1)} collective-permute-done((f32[512,640]{1,0:T(8,128)}, f32[512,640]{1,0:T(8,128)S(1)}, u32[]{:S(2)}, u32[]{:S(2)}) %collective-permute-start.11) | collective-permute-done | bytes 1310752 | tf_op jit(solution)/shard_map/ppermute | solution.py:431
  103.0 1.8 %shard_map.34 = f32[512,640]{1,0:T(8,128)} custom-call(s32[7]{0:T(128)S(1)} %stack.39.role, s32[512,1]{1,0:T(8,128)S(1)} %fusion.row_cohort, s32[1,640]{1,0:T(1,128)S(1)} %and_select_fusion.col_cohort, f32[512,640]{1,0:T(8,128)S(1)} %get-tuple-element.35.keep, f32[512,640]{1,0:T(8,128)S(1)} %collective-permute-done.11.came), custom_call_target="tpu_custom_call" | custom-call | tf_op jit(solution)/shard_map/pallas_call | solution.py:477
  (9 shorter events, 0.1 us)
Async XLA Ops:
  0.0 34.6 %collective-permute-start.1 = (bf16[3,512,768]{2,1,0:T(8,128)(2,1)}, bf16[3,512,768]{2,1,0:T(8,128)(2,1)S(1)}, u32[]{:S(2)}, u32[]{:S(2)}) collective-permute-start(bf16[3,512,768]{2,1,0:T(8,128)(2,1)} %own.1), channel_id=1, source_target_pairs={{1,9},{3,11},{5,13},{7,15},{8,0},{9,17},{10,2},{11,19},{12,4},{13,... | collective-permute-start | bytes 7077896 | tf_op jit(solution)/shard_map/ppermute | solution.py:431
  3.5 38.5 %collective-permute-start = (bf16[3,512,768]{2,1,0:T(8,128)(2,1)}, bf16[3,512,768]{2,1,0:T(8,128)(2,1)}, u32[]{:S(2)}, u32[]{:S(2)}) collective-permute-start(bf16[3,512,768]{2,1,0:T(8,128)(2,1)} %own.1), channel_id=1, source_target_pairs={{0,1},{1,5},{2,3},{3,7},{4,0},{5,4},{6,2},{7,6},{8,9},{9,13},{10,1... | collective-permute-start | bytes 7077896 | tf_op jit(solution)/shard_map/ppermute | solution.py:431
  19.4 1.7 %copy-start = (bf16[3,512,768]{2,1,0:T(8,128)(2,1)S(1)}, bf16[3,512,768]{2,1,0:T(8,128)(2,1)}, u32[]{:S(2)}) copy-start(bf16[3,512,768]{2,1,0:T(8,128)(2,1)} %own.1) | copy-start | bytes 7077892
  36.8 16.9 %collective-permute-start.2 = (f32[2,512,256]{2,1,0:T(8,128)S(1)}, f32[2,512,256]{2,1,0:T(8,128)S(1)}, u32[]{:S(2)}, u32[]{:S(2)}) collective-permute-start(f32[2,512,256]{2,1,0:T(8,128)S(1)} %shard_map.30.after), channel_id=1, source_target_pairs={{4,13},{6,15},{9,0},{11,2},{12,21},{14,23},{17,8},{19,10},{20,29},... | collective-permute-start | bytes 3145736 | tf_op jit(solution)/shard_map/ppermute | solution.py:431
  43.7 11.2 %collective-permute-start.6 = (f32[2,256,512]{2,1,0:T(8,128)S(1)}, f32[2,256,512]{2,1,0:T(8,128)S(1)}, u32[]{:S(2)}, u32[]{:S(2)}) collective-permute-start(f32[2,256,512]{2,1,0:T(8,128)S(1)} %get-tuple-element.32), channel_id=1, source_target_pairs={{0,2},{2,0},{5,7},{7,5},{8,10},{10,8},{13,15},{15,13},{16,18},{18,... | collective-permute-start | bytes 3145736 | tf_op jit(solution)/shard_map/ppermute | solution.py:431
  54.2 2.4 %collective-permute-start.3 = (f32[2,256,512]{2,1,0:T(8,128)S(1)}, f32[2,256,512]{2,1,0:T(8,128)S(1)}, u32[]{:S(2)}, u32[]{:S(2)}) collective-permute-start(f32[2,256,512]{2,1,0:T(8,128)S(1)} %get-tuple-element.28), channel_id=1, source_target_pairs={{0,2},{2,0},{5,7},{7,5},{8,10},{10,8},{13,15},{15,13},{16,18},{18,... | collective-permute-start | bytes 3145736 | tf_op jit(solution)/shard_map/ppermute | solution.py:431
  55.2 24.9 %collective-permute-start.7 = (f32[2,256,512]{2,1,0:T(8,128)S(1)}, f32[2,256,512]{2,1,0:T(8,128)S(1)}, u32[]{:S(2)}, u32[]{:S(2)}) collective-permute-start(f32[2,256,512]{2,1,0:T(8,128)S(1)} %add.98.full_a), channel_id=1, source_target_pairs={{0,8},{8,16},{15,7},{16,24},{23,15},{24,32},{31,23},{32,40},{39,31... | collective-permute-start | bytes 3145736 | tf_op jit(solution)/shard_map/ppermute | solution.py:431
  55.9 26.9 %collective-permute-start.9 = (f32[2,256,512]{2,1,0:T(8,128)S(1)}, f32[2,256,512]{2,1,0:T(8,128)S(1)}, u32[]{:S(2)}, u32[]{:S(2)}) collective-permute-start(f32[2,256,512]{2,1,0:T(8,128)S(1)} %add.98.full_a), channel_id=1, source_target_pairs={{0,7},{2,5},{5,2},{7,0},{8,15},{10,13},{13,10},{15,8},{16,23},{18,... | collective-permute-start | bytes 3145736 | tf_op jit(solution)/shard_map/ppermute | solution.py:431
  56.9 25.9 %collective-permute-start.10 = (f32[2,256,512]{2,1,0:T(8,128)S(1)}, f32[2,256,512]{2,1,0:T(8,128)S(1)}, u32[]{:S(2)}, u32[]{:S(2)}) collective-permute-start(f32[2,256,512]{2,1,0:T(8,128)S(1)} %add.99.full_b), channel_id=1, source_target_pairs={{0,7},{2,5},{5,2},{7,0},{8,15},{10,13},{13,10},{15,8},{16,23},{18,... | collective-permute-start | bytes 3145736 | tf_op jit(solution)/shard_map/ppermute | solution.py:431
  57.6 25.2 %collective-permute-start.8 = (f32[2,256,512]{2,1,0:T(8,128)S(1)}, f32[2,256,512]{2,1,0:T(8,128)S(1)}, u32[]{:S(2)}, u32[]{:S(2)}) collective-permute-start(f32[2,256,512]{2,1,0:T(8,128)S(1)} %add.99.full_b), channel_id=1, source_target_pairs={{0,8},{8,16},{15,7},{16,24},{23,15},{24,32},{31,23},{32,40},{39,31... | collective-permute-start | bytes 3145736 | tf_op jit(solution)/shard_map/ppermute | solution.py:431
  58.4 33.3 %collective-permute-start.4 = (f32[2,512,256]{2,1,0:T(8,128)S(1)}, f32[2,512,256]{2,1,0:T(8,128)S(1)}, u32[]{:S(2)}, u32[]{:S(2)}) collective-permute-start(f32[2,512,256]{2,1,0:T(8,128)S(1)} %get-tuple-element.29), channel_id=1, source_target_pairs={{1,2},{3,0},{4,7},{6,5},{9,10},{11,8},{12,15},{14,13},{17,18},{19,... | collective-permute-start | bytes 3145736 | tf_op jit(solution)/shard_map/ppermute | solution.py:431
  80.1 11.7 %collective-permute-start.5 = (f32[2,512,256]{2,1,0:T(8,128)S(1)}, f32[2,512,256]{2,1,0:T(8,128)S(1)}, u32[]{:S(2)}, u32[]{:S(2)}) collective-permute-start(f32[2,512,256]{2,1,0:T(8,128)S(1)} %get-tuple-element.30), channel_id=1, source_target_pairs={{1,0},{3,2},{4,5},{6,7},{9,8},{11,10},{12,13},{14,15},{17,16},{19,... | collective-permute-start | bytes 3145736 | tf_op jit(solution)/shard_map/ppermute | solution.py:431
  93.3 9.7 %collective-permute-start.11 = (f32[512,640]{1,0:T(8,128)}, f32[512,640]{1,0:T(8,128)S(1)}, u32[]{:S(2)}, u32[]{:S(2)}) collective-permute-start(f32[512,640]{1,0:T(8,128)} %get-tuple-element.36), channel_id=1, source_target_pairs={{0,1},{2,3},{5,4},{7,6},{8,9},{10,11},{13,12},{15,14},{16,17},{18,... | collective-permute-start | bytes 3932168 | tf_op jit(solution)/shard_map/ppermute | solution.py:431

commit v4 on v3

--- a/solution.py
+++ b/solution.py
@@ -148,33 +148,53 @@
         put_tiles(tri, far_v, own, par, beyond)
 
 
-def first_kernel(role, own, own_obs, mate, far, after, send_a, send_b, far_v, sems):
+def chunk(data, start):
+    at = pl.ds(pl.multiple_of(start, HALF), HALF)
+    return [data[plane, at, :] for plane in range(3)]
+
+
+def first_kernel(role, own, own_obs, mate, far, after, send_a, mate_obs, far_v, sems):
     par, lo, core = role[0], role[1], role[2]
     kind_a = core == par
     outer = lo == par
+    start = jnp.where(outer == (par == 0), HALF, 0)
+
+    def put(left_rows, left_obs):
+        num, den = pair_sums(left_rows, left_obs, mate, mate_obs[...])
+        send_a[0] = num
+        send_a[1] = den
 
     @pl.when(kind_a & outer)
     def _():
-        put_rows(send_a, send_b, pair_sums(own, own_obs[...], mate, observed(mate)), par == 0)
+        mate_obs[...] = observed(mate)
+        left_rows = chunk(own, start)
+        put(left_rows, observed(left_rows))
 
     @pl.when(kind_a & jnp.logical_not(outer))
     def _():
-        fetch(far, far_v, sems)
-        mate_obs = observed(mate)
-        arrived(far, far_v, sems, 1)
-        same = dot_t(far_v[1], mate[1])
-        den = dot_t(far_v[1], mate_obs)
-        arrived(far, far_v, sems, 0)
-        cross = dot_t(far_v[0], mate[2])
-        arrived(far, far_v, sems, 2)
-        cross = cross + dot_t(far_v[2], mate[0])
-        den = den + dot_t(observed(far_v), mate[1])
-        put_rows(send_a, send_b, (same - 2.0 * cross, den), par == 1)
-
-
-def second_kernel(role, own, own_obs, mate, far, keep_a, keep_b, tri, send_d, keep_d, far_v, sems):
+        at = pl.ds(pl.multiple_of(start, HALF), HALF)
+        copies = [
+            pltpu.make_async_copy(far.at[plane, at], far_v.at[plane], sems.at[plane]) for plane in range(3)
+        ]
+        for copy in copies:
+            copy.start()
+        mate_obs[...] = observed(mate)
+        for copy in copies:
+            copy.wait()
+        put(far_v, observed(far_v))
+
+
+def second_kernel(
+    role, own, own_obs, mate, mate_obs, far, held_b, keep_a, keep_b, tri, send_d, keep_d, far_v, sems
+):
     par, lo, core, beyond = role[0], role[1], role[2], role[3]
     outer = lo == par
+
+    def rest(left, start):
+        left_rows = chunk(left, start)
+        num, den = pair_sums(left_rows, observed(left_rows), mate, mate_obs[...])
+        held_b[0] = num
+        held_b[1] = den
 
     @pl.when(core == par)
     def _():
@@ -185,17 +205,19 @@
 
         @pl.when(outer)
         def _():
-            put_rows(keep_a, keep_b, pair_sums(far_v, observed(far_v), mate, observed(mate)), par == 1)
+            rest(own, jnp.where(par == 0, 0, HALF))
+            put_rows(keep_a, keep_b, pair_sums(far_v, observed(far_v), mate, mate_obs[...]), par == 1)
 
         @pl.when(jnp.logical_not(outer))
         def _():
-            put_rows(keep_a, keep_b, pair_sums(own, own_obs[...], mate, observed(mate)), par == 0)
+            rest(far_v, jnp.where(par == 1, 0, HALF))
+            put_rows(keep_a, keep_b, pair_sums(own, own_obs[...], mate, mate_obs[...]), par == 0)
 
     @pl.when(core != par)
     def _():
         first = pair_sums(own, own_obs[...], own, own_obs[...])
-        mate_obs = observed(mate)
-        second = pair_sums(mate, mate_obs, mate, mate_obs)
+        twin_obs = observed(mate)
+        second = pair_sums(mate, twin_obs, mate, twin_obs)
         diag = (first[0] + second[0], first[1] + second[1])
 
         @pl.when(lo == 0)
@@ -265,35 +287,19 @@
     return num / jnp.maximum(den, 1.0)
 
 
-def ratio_kernel(role, diag_in, diag, cut_a, cut_b, mirror_a, mirror_b, full_a, full_b, send, keep):
+def ordered(first, second, i, swap):
+    pair = (second[i], first[i]) if swap else (first[i], second[i])
+    return jnp.concatenate(pair, axis=0)
+
+
+def early_kernel(role, diag_in, diag, cut_a, cut_b, full_a, full_b, mirror_a, part, done, mine, other):
     par, lo, core, beyond = role[0], role[1], role[2], role[4]
-    kind_a = core == par
-    outer = lo == par
-
-    def ordered(first, second, i, swap):
-        pair = (second[i], first[i]) if swap else (first[i], second[i])
-        return jnp.concatenate(pair, axis=0)
-
-    def behind(parity):
-        flip = parity == 1
-        num, den = [
-            ordered(cut_a, cut_b, i, flip) + ordered(mirror_a, mirror_b, i, not flip).T
-            for i in range(2)
-        ]
-        return ratio(num, den)
-
-    def ahead(parity):
-        flip = parity == 0
-        num, den = [
-            ordered(full_a, full_b, i, flip) + ordered(mirror_a, mirror_b, i, not flip).T
-            for i in range(2)
-        ]
-        return ratio(num, den)
-
-    def put_diag(target, start):
-        target[:, start : start + HALF] = ratio(diag[0] + diag_in[0], diag[1] + diag_in[1])
-
-    def put_tiles_at(target, start, parity, source, flip):
+    outer = lo == par
+
+    def put_diag(target):
+        target[:, :HALF] = ratio(diag[0] + diag_in[0], diag[1] + diag_in[1])
+
+    def put_tiles_at(target, parity, source, flip):
         near_x = HALF if parity == 0 else 0
         near_z = HALF - near_x
         both = near_z if flip else near_x
@@ -304,7 +310,7 @@
 
         def place(x, z, value):
             row, col = (z, x) if flip else (x, z)
-            target[row : row + HALF, start + col : start + col + HALF] = value
+            target[row : row + HALF, col : col + HALF] = value
 
         zero = jnp.zeros((HALF, HALF), F32)
         place(near_x, near_z, first)
@@ -320,52 +326,92 @@
             place(HALF - near_x, near_z, second)
             place(near_x, HALF - near_z, zero)
 
+    def put_sums(sums, swap):
+        at, rest = slice(0, HALF), slice(HALF, TILE)
+        if swap:
+            at, rest = rest, at
+        done[...] = ratio(sums[0][:, at] + mirror_a[0].T, sums[1][:, at] + mirror_a[1].T)
+        part[0] = sums[0][:, rest]
+        part[1] = sums[1][:, rest]
+
     def when(parity, want_outer):
-        return pl.when((par == parity) & kind_a & (outer == want_outer))
+        return pl.when((par == parity) & (core == par) & (outer == want_outer))
+
+    for parity in range(2):
+
+        @when(parity, True)
+        def _():
+            put_sums([ordered(cut_a, cut_b, i, parity == 1) for i in range(2)], parity == 0)
+            put_tiles_at(mine, parity, cut_b, True)
+            put_diag(other)
+
+        @when(parity, False)
+        def _():
+            put_sums([ordered(full_a, full_b, i, parity == 0) for i in range(2)], parity == 1)
+            put_tiles_at(other, parity, full_b, False)
+            put_diag(mine)
+
+
+def ratio_kernel(role, part, done, mirror_b, send, keep):
+    par, lo, core = role[0], role[1], role[2]
+    outer = lo == par
+
+    def when(parity, want_outer):
+        return pl.when((par == parity) & (core == par) & (outer == want_outer))
+
+    def value(parity, from_outer):
+        swap = (parity == 0) == from_outer
+        last = ratio(part[0] + mirror_b[0].T, part[1] + mirror_b[1].T)
+        return jnp.concatenate([last, done[...]] if swap else [done[...], last], axis=1)
 
     @when(0, True)
     def _():
-        value = behind(0)
-        put_tiles_at(keep, 0, 0, cut_b, True)
-        keep[:, 512:] = value[:, :128]
-        send[:, :384] = value[:, 128:]
-        put_diag(send, 384)
+        result = value(0, True)
+        keep[:, :128] = result[:, :128]
+        send[...] = result[:, 128:]
 
     @when(1, True)
     def _():
-        value = behind(1)
-        keep[:, :128] = value[:, 384:]
-        put_tiles_at(keep, 128, 1, cut_b, True)
-        put_diag(send, 0)
-        send[:, 256:] = value[:, :384]
+        result = value(1, True)
+        keep[:, :128] = result[:, 384:]
+        send[...] = result[:, :384]
 
     @when(0, False)
     def _():
-        value = ahead(0)
-        put_diag(keep, 0)
-        keep[:, 256:] = value[:, :384]
-        send[:, :128] = value[:, 384:]
-        put_tiles_at(send, 128, 0, full_b, False)
+        result = value(0, False)
+        keep[...] = result[:, :384]
+        send[:, :128] = result[:, 384:]
 
     @when(1, False)
     def _():
-        value = ahead(1)
-        put_tiles_at(send, 0, 1, full_b, False)
-        send[:, 512:] = value[:, :128]
-        keep[:, :384] = value[:, 128:]
-        put_diag(keep, 384)
-
-
-def place_kernel(role, row_cohort, col_cohort, keep, came, out):
-    same = row_cohort[...] == col_cohort[...]
-
-    @pl.when(role[2] == role[0])
-    def _():
-        out[...] = jnp.where(same, keep[...], 0.0)
-
-    @pl.when(role[2] != role[0])
-    def _():
-        out[...] = jnp.where(same, came[...], 0.0)
+        result = value(1, False)
+        keep[...] = result[:, 128:]
+        send[:, :128] = result[:, :128]
+
+
+def place_kernel(role, row_cohort, col_cohort, keep, came, mine, other, out):
+    par, lo, core = role[0], role[1], role[2]
+    kind_a = core == par
+    outer = lo == par
+    rows = row_cohort[...]
+
+    def when(parity, want_a, want_outer, parts):
+        @pl.when((par == parity) & (kind_a == want_a) & (outer == want_outer))
+        def _():
+            start = 0
+            for ref, width in parts:
+                same = rows == col_cohort[:, start : start + width]
+                out[:, start : start + width] = jnp.where(same, ref[:, :width], 0.0)
+                start += width
+
+    when(0, True, True, [(mine, 512), (keep, 128)])
+    when(0, False, True, [(came, 384), (other, 256)])
+    when(0, True, False, [(mine, 256), (keep, 384)])
+    when(0, False, False, [(came, 128), (other, 512)])
+    when(1, False, False, [(other, 512), (came, 128)])
+    when(1, True, False, [(keep, 384), (mine, 256)])
+    when(1, False, True, [(other, 256), (came, 384)])
+    when(1, True, True, [(keep, 128), (mine, 512)])
 
 
 def cohort_of(positions, cohort_ends):
@@ -442,17 +488,18 @@
         role, probs
     )
     send_t = call(tiles_kernel, half, (vmem, pl.ANY), (block_of, planes))(role, own, far)
-    send_a, held_b = call(
-        first_kernel, (rows, rows), (vmem, vmem, vmem, pl.ANY, pl.ANY), (block_of, planes)
+    chunk_of = pltpu.VMEM((3, HALF, probs.shape[2]), probs.dtype)
+    send_a, mate_obs = call(
+        first_kernel, (rows, obs), (vmem, vmem, vmem, pl.ANY, pl.ANY), (chunk_of, planes)
     )(role, own, own_obs, mate, far, send_t)
     tri_in = move(send_t, to_far)
     came_a = move(send_a, to_chip)
-    keep_a, kept_b, tri, send_d, keep_d = call(
+    held_b, keep_a, kept_b, tri, send_d, keep_d = call(
         second_kernel,
-        (rows, rows, half, half, half),
-        (vmem, vmem, vmem, pl.ANY),
+        (rows, rows, rows, half, half, half),
+        (vmem, vmem, vmem, vmem, pl.ANY),
         (block_of, planes),
-    )(role, own, own_obs, mate, far)
+    )(role, own, own_obs, mate, mate_obs, far)
     send_b, keep_b = call(merge_kernel, (rows, rows), [pltpu.VMEM] * 4)(role, held_b, kept_b, tri, tri_in)
     came_b = move(send_b, to_chip)
     full_a = keep_a + came_a
@@ -465,16 +512,23 @@
     mirror_b = move(full_b, to_mirror)
     diag = move(keep_d, to_side)
     wide = jax.ShapeDtypeStruct((TILE, WIDTH), F32)
-    send, keep = call(ratio_kernel, (wide, wide), [pltpu.VMEM] * 8)(
-        role, diag_in, diag, cut_a, cut_b, mirror_a, mirror_b, full_a, full_b
+    square = jax.ShapeDtypeStruct((TILE, TILE), F32)
+    column = jax.ShapeDtypeStruct((TILE, HALF), F32)
+    narrow = jax.ShapeDtypeStruct((TILE, 384), F32)
+    part, done, mine, other = call(early_kernel, (half, column, square, square), [vmem] * 7)(
+        role, diag_in, diag, cut_a, cut_b, full_a, full_b, mirror_a
     )
+    other = move(other, to_core)
+    send, keep = call(ratio_kernel, (narrow, narrow), [vmem] * 3)(role, part, done, mirror_b)
     came = move(send, to_core)
 
     col_pos = (block - 2) * TILE + quarter * WIDTH + jnp.arange(WIDTH, dtype=jnp.int32)
     inside = (col_pos >= 0) & (col_pos < TILE * blocks)
     row_cohort = own_ids[:, None]
     col_cohort = jnp.where(inside, cohort_of(col_pos, cohort_ends), -1)[None, :]
-    return call(place_kernel, wide, [pltpu.VMEM] * 4)(role, row_cohort, col_cohort, keep, came)
+    return call(place_kernel, wide, [vmem] * 6)(
+        role, row_cohort, col_cohort, keep, came, mine, other
+    )
 
 
 def solution(mesh):

time: 106 us -> 104 us (0.981)
  starting transfers between devices: 41.8 us -> 38.2 us
  Pallas kernels: 15.2 us -> 17.2 us
    ppermute x12 -> x13, starting transfers between devices: 41.8 us -> 38.2 us  [move(): return lax.ppermute(value, AXES, route(blocks, rule))]
    pallas_call x4 -> x5, Pallas kernels: 11.5 us -> 13.4 us  [the longest x1 6.32 us: per_device(): call(second_kernel, (rows, rows, rows, half, half, half), (vmem, vmem, vm...]
    ppermute x12 -> x13, waiting for transfers between devices: 32.3 us -> 32.6 us  [move(): return lax.ppermute(value, AXES, route(blocks, rule))]
  transfers between devices with their start and end apart: 12 -> 13, of which waited for: 4 -> 4; matrix products, arithmetic and copies ran while one was open for 7% -> 7% of each run, Pallas kernels for 11% -> 14%
where the time goes in v4:
time: 104 us; the launch traced here: 103 us
  starting transfers between devices  38.2 us (37%)
  waiting for transfers between devices  32.6 us (31%)
  Pallas kernels  17.2 us (17%)
  between operations  6.69 us (6%)
  local copies, waits for them, and re-layouts  5.86 us (6%)
  other arithmetic  2.93 us (3%)
    ppermute x13, starting transfers between devices, move(): return lax.ppermute(value, AXES, route(blocks, rule))  38.2 us
    ppermute x13, waiting for transfers between devices, move(): return lax.ppermute(value, AXES, route(blocks, rule))  32.6 us
    pallas_call x1, Pallas kernels, per_device(): call(second_kernel, (rows, rows, rows, half, half, half), (vmem, vmem, vm...  6.32 us
    pallas_call x1, Pallas kernels, per_device(): call(place_kernel, wide, [vmem] * 6)  2.4 us
    pallas_call x1, Pallas kernels, per_device(): call(tiles_kernel, half, (vmem, pl.ANY), (block_of, planes))(role, own, far)  2.21 us
  transfers between devices with their start and end apart: 13, of which 4 were waited for; matrix products, arithmetic and copies ran while one was open for 7% of the time, Pallas kernels for 14%

profile of v4, /device:TPU:7, one launch (start us, length us, event | category | flops | bytes accessed | tf_op | source)
XLA Modules:
  0.0 103.4 jit_solution(2748857826885951522)
XLA Ops:
  0.0 3.5 %collective-permute-start.1 = (bf16[3,512,768]{2,1,0:T(8,128)(2,1)}, bf16[3,512,768]{2,1,0:T(8,128)(2,1)S(1)}, u32[]{:S(2)}, u32[]{:S(2)}) collective-permute-start(bf16[3,512,768]{2,1,0:T(8,128)(2,1)} %own.1), channel_id=1, source_target_pairs={{1,9},{3,11},{5,13},{7,15},{8,0},{9,17},{10,2},{11,19},{12,4},{13,... | collective-permute-start | bytes 7077896 | tf_op jit(solution)/shard_map/ppermute | solution.py:477
  3.5 3.0 %collective-permute-start = (bf16[3,512,768]{2,1,0:T(8,128)(2,1)}, bf16[3,512,768]{2,1,0:T(8,128)(2,1)}, u32[]{:S(2)}, u32[]{:S(2)}) collective-permute-start(bf16[3,512,768]{2,1,0:T(8,128)(2,1)} %own.1), channel_id=1, source_target_pairs={{0,1},{1,5},{2,3},{3,7},{4,0},{5,4},{6,2},{7,6},{8,9},{9,13},{10,1... | collective-permute-start | bytes 7077896 | tf_op jit(solution)/shard_map/ppermute | solution.py:477
  6.5 0.8 copy.6
  7.3 0.1 reduce-window.8
  7.4 0.1 reduce
  7.5 0.1 convert_reduce_fusion.1
  7.7 0.7 fusion.5
  9.7 0.7 fusion.4
  11.6 0.7 compare_reduce_fusion
  14.8 0.7 fusion.3
  16.7 0.7 fusion.1
  17.5 0.6 fusion.2
  18.1 1.3 %stack.39.role = s32[7]{0:T(128)S(1)} concatenate(s32[1]{0:T(128)} %bitcast, s32[1]{0:T(128)} %bitcast.1, s32[1]{0:T(128)} %bitcast.2, s32[1]{0:T(128)} %bitcast.8, s32[1]{0:T(128)} %bitcast.9, s32[1]{0:T(128)} %bitcast.10, s32[1]{0:T(128)} %bitcast.13), dimensions={0} | concatenate | bytes 56 | tf_op jit(solution)/shard_map/stack | solution.py:464
  19.4 0.0 copy-start
  19.4 1.7 %copy-done = bf16[3,512,768]{2,1,0:T(8,128)(2,1)S(1)} copy-done((bf16[3,512,768]{2,1,0:T(8,128)(2,1)S(1)}, bf16[3,512,768]{2,1,0:T(8,128)(2,1)}, u32[]{:S(2)}) %copy-start) | copy-done | bytes 2359320
  21.1 1.0 shard_map.28
  22.0 12.5 %collective-permute-done.1.far = bf16[3,512,768]{2,1,0:T(8,128)(2,1)S(1)} collective-permute-done((bf16[3,512,768]{2,1,0:T(8,128)(2,1)}, bf16[3,512,768]{2,1,0:T(8,128)(2,1)S(1)}, u32[]{:S(2)}, u32[]{:S(2)}) %collective-permute-start.1) | collective-permute-done | bytes 2359328 | tf_op jit(solution)/shard_map/ppermute | solution.py:477
  34.6 2.2 %shard_map.29.after = f32[2,512,256]{2,1,0:T(8,128)S(1)} custom-call(s32[7]{0:T(128)S(1)} %stack.39.role, bf16[3,512,768]{2,1,0:T(8,128)(2,1)S(1)} %get-tuple-element.26.own, bf16[3,512,768]{2,1,0:T(8,128)(2,1)S(1)} %collective-permute-done.1.far), custom_call_target="tpu_custom_call" | custom-call | tf_op jit(solution)/shard_map/pallas_call | solution.py:490
  36.8 5.2 %collective-permute-start.2 = (f32[2,512,256]{2,1,0:T(8,128)S(1)}, f32[2,512,256]{2,1,0:T(8,128)S(1)}, u32[]{:S(2)}, u32[]{:S(2)}) collective-permute-start(f32[2,512,256]{2,1,0:T(8,128)S(1)} %shard_map.29.after), channel_id=1, source_target_pairs={{4,13},{6,15},{9,0},{11,2},{12,21},{14,23},{17,8},{19,10},{20,29},... | collective-permute-start | bytes 3145736 | tf_op jit(solution)/shard_map/ppermute | solution.py:477
  42.0 0.0 collective-permute-done.mate
  42.0 1.7 %shard_map.30 = (f32[2,256,512]{2,1,0:T(8,128)S(1)}, bf16[512,768]{1,0:T(8,128)(2,1)S(1)}) custom-call(s32[7]{0:T(128)S(1)} %stack.39.role, bf16[3,512,768]{2,1,0:T(8,128)(2,1)S(1)} %get-tuple-element.26.own, bf16[512,768]{1,0:T(8,128)(2,1)S(1)} %get-tuple-element.27.own_obs, bf16[3,512,768]{2,1,0:T(8,128)(2,1)} %collective-permute-done.mate, ...), custom_call_target="tpu_custom_call" | custom-call | tf_op jit(solution)/shard_map/pallas_call | solution.py:492
  43.7 0.7 collective-permute-start.6
  44.5 6.3 %shard_map.31 = (f32[2,256,512]{2,1,0:T(8,128)S(1)}, f32[2,256,512]{2,1,0:T(8,128)S(1)}, f32[2,256,512]{2,1,0:T(8,128)S(1)}, f32[2,512,256]{2,1,0:T(8,128)S(1)},...) custom-call(s32[7]{0:T(128)S(1)} %stack.39.role, bf16[3,512,768]{2,1,0:T(8,128)(2,1)S(1)} %get-tuple-element.26.own, ...), custom_call_target="tpu_custom_call" | custom-call | tf_op jit(solution)/shard_map/pallas_call | solution.py:497
  50.8 2.9 %collective-permute-done.2.tri_in = f32[2,512,256]{2,1,0:T(8,128)S(1)} collective-permute-done((f32[2,512,256]{2,1,0:T(8,128)S(1)}, f32[2,512,256]{2,1,0:T(8,128)S(1)}, u32[]{:S(2)}, u32[]{:S(2)}) %collective-permute-start.2) | collective-permute-done | bytes 1048608 | tf_op jit(solution)/shard_map/ppermute | solution.py:477
  53.7 0.6 shard_map.32
  54.2 0.7 collective-permute-start.3
  55.0 0.0 collective-permute-done.6
  55.0 0.2 add.98.full_a
  55.2 0.7 collective-permute-start.7
  55.9 0.7 collective-permute-start.9
  56.7 0.0 collective-permute-done.3
  56.7 0.2 add.99.full_b
  56.9 0.7 collective-permute-start.8
  57.6 17.6 %collective-permute-start.4 = (f32[2,512,256]{2,1,0:T(8,128)S(1)}, f32[2,512,256]{2,1,0:T(8,128)S(1)}, u32[]{:S(2)}, u32[]{:S(2)}) collective-permute-start(f32[2,512,256]{2,1,0:T(8,128)S(1)} %get-tuple-element.35), channel_id=1, source_target_pairs={{1,2},{3,0},{4,7},{6,5},{9,10},{11,8},{12,15},{14,13},{17,18},{19,... | collective-permute-start | bytes 3145736 | tf_op jit(solution)/shard_map/ppermute | solution.py:477
  75.3 1.9 %collective-permute-start.5 = (f32[2,512,256]{2,1,0:T(8,128)S(1)}, f32[2,512,256]{2,1,0:T(8,128)S(1)}, u32[]{:S(2)}, u32[]{:S(2)}) collective-permute-start(f32[2,512,256]{2,1,0:T(8,128)S(1)} %get-tuple-element.36), channel_id=1, source_target_pairs={{1,0},{3,2},{4,5},{6,7},{9,8},{11,10},{12,13},{14,15},{17,16},{19,... | collective-permute-start | bytes 3145736 | tf_op jit(solution)/shard_map/ppermute | solution.py:477
  77.2 0.0 collective-permute-done.7.cut_a
  77.2 0.7 collective-permute-start.10
  77.9 0.0 collective-permute-done.9.mirror_a
  77.9 0.0 collective-permute-done.8.cut_b
  77.9 9.0 %collective-permute-done.4.diag_in = f32[2,512,256]{2,1,0:T(8,128)S(1)} collective-permute-done((f32[2,512,256]{2,1,0:T(8,128)S(1)}, f32[2,512,256]{2,1,0:T(8,128)S(1)}, u32[]{:S(2)}, u32[]{:S(2)}) %collective-permute-start.4) | collective-permute-done | bytes 1048608 | tf_op jit(solution)/shard_map/ppermute | solution.py:477
  86.9 0.0 collective-permute-done.5.diag
  86.9 1.5 %shard_map.33 = (f32[2,512,256]{2,1,0:T(8,128)S(1)}, f32[512,256]{1,0:T(8,128)S(1)}, f32[512,512]{1,0:T(8,128)S(1)}, f32[512,512]{1,0:T(8,128)}) custom-call(s32[7]{0:T(128)S(1)} %stack.39.role, f32[2,512,256]{2,1,0:T(8,128)S(1)} %collective-permute-done.4.diag_in, f32[2,512,256]{2,1,0:T(8,128)S(1)} %collective-permute-done.5.diag, ...), custom_call_target="tpu_custom_call" | custom-call | tf_op jit(solution)/shard_map/pallas_call | solution.py:518
  88.5 1.3 %collective-permute-start.12 = (f32[512,512]{1,0:T(8,128)}, f32[512,512]{1,0:T(8,128)S(1)}, u32[]{:S(2)}, u32[]{:S(2)}) collective-permute-start(f32[512,512]{1,0:T(8,128)} %get-tuple-element.46), channel_id=1, source_target_pairs={{0,1},{2,3},{5,4},{7,6},{8,9},{10,11},{13,12},{15,14},{16,17},{18,... | collective-permute-start | bytes 3145736 | tf_op jit(solution)/shard_map/ppermute | solution.py:477
  89.8 0.0 collective-permute-done.10.mirror_b
  89.8 1.4 %shard_map.34 = (f32[512,384]{1,0:T(8,128)}, f32[512,384]{1,0:T(8,128)S(1)}) custom-call(s32[7]{0:T(128)S(1)} %stack.39.role, f32[2,512,256]{2,1,0:T(8,128)S(1)} %get-tuple-element.41.part, f32[512,256]{1,0:T(8,128)S(1)} %get-tuple-element.42.done, f32[2,256,512]{2,1,0:T(8,128)S(1)} %collective-permute-done.10.mirror_b), custom_call_target="tpu_custom_call" | custom-call | tf_op jit(solution)/shard_map/pallas_call | solution.py:522
  91.2 1.3 %collective-permute-start.11 = (f32[512,384]{1,0:T(8,128)}, f32[512,384]{1,0:T(8,128)}, u32[]{:S(2)}, u32[]{:S(2)}) collective-permute-start(f32[512,384]{1,0:T(8,128)} %get-tuple-element.44), channel_id=1, source_target_pairs={{0,1},{2,3},{5,4},{7,6},{8,9},{10,11},{13,12},{15,14},{16,17},{18,... | collective-permute-start | bytes 2359304 | tf_op jit(solution)/shard_map/ppermute | solution.py:477
  92.5 0.1 copy.7
  92.7 0.1 convert_reduce_fusion
  92.8 8.2 %collective-permute-done.11.came = f32[512,384]{1,0:T(8,128)} collective-permute-done((f32[512,384]{1,0:T(8,128)}, f32[512,384]{1,0:T(8,128)}, u32[]{:S(2)}, u32[]{:S(2)}) %collective-permute-start.11) | collective-permute-done | bytes 786464 | tf_op jit(solution)/shard_map/ppermute | solution.py:477
  101.0 0.0 collective-permute-done.12.other
  101.0 2.4 %shard_map.35 = f32[512,640]{1,0:T(8,128)} custom-call(s32[7]{0:T(128)S(1)} %stack.39.role, s32[512,1]{1,0:T(8,128)S(1)} %fusion.row_cohort, s32[1,640]{1,0:T(1,128)S(1)} %and_select_fusion.col_cohort, f32[512,384]{1,0:T(8,128)S(1)} %get-tuple-element.43.keep, f32[512,384]{1,0:T(8,128)} %collective-permute-done.11.came, ...), custom_call_target="tpu_custom_call" | custom-call | tf_op jit(solution)/shard_map/pallas_call | solution.py:529
  (9 shorter events, 0.1 us)
Async XLA Ops:
  0.0 34.6 %collective-permute-start.1 = (bf16[3,512,768]{2,1,0:T(8,128)(2,1)}, bf16[3,512,768]{2,1,0:T(8,128)(2,1)S(1)}, u32[]{:S(2)}, u32[]{:S(2)}) collective-permute-start(bf16[3,512,768]{2,1,0:T(8,128)(2,1)} %own.1), channel_id=1, source_target_pairs={{1,9},{3,11},{5,13},{7,15},{8,0},{9,17},{10,2},{11,19},{12,4},{13,... | collective-permute-start | bytes 7077896 | tf_op jit(solution)/shard_map/ppermute | solution.py:477
  3.5 38.5 %collective-permute-start = (bf16[3,512,768]{2,1,0:T(8,128)(2,1)}, bf16[3,512,768]{2,1,0:T(8,128)(2,1)}, u32[]{:S(2)}, u32[]{:S(2)}) collective-permute-start(bf16[3,512,768]{2,1,0:T(8,128)(2,1)} %own.1), channel_id=1, source_target_pairs={{0,1},{1,5},{2,3},{3,7},{4,0},{5,4},{6,2},{7,6},{8,9},{9,13},{10,1... | collective-permute-start | bytes 7077896 | tf_op jit(solution)/shard_map/ppermute | solution.py:477
  19.4 1.7 %copy-start = (bf16[3,512,768]{2,1,0:T(8,128)(2,1)S(1)}, bf16[3,512,768]{2,1,0:T(8,128)(2,1)}, u32[]{:S(2)}) copy-start(bf16[3,512,768]{2,1,0:T(8,128)(2,1)} %own.1) | copy-start | bytes 7077892
  36.8 16.9 %collective-permute-start.2 = (f32[2,512,256]{2,1,0:T(8,128)S(1)}, f32[2,512,256]{2,1,0:T(8,128)S(1)}, u32[]{:S(2)}, u32[]{:S(2)}) collective-permute-start(f32[2,512,256]{2,1,0:T(8,128)S(1)} %shard_map.29.after), channel_id=1, source_target_pairs={{4,13},{6,15},{9,0},{11,2},{12,21},{14,23},{17,8},{19,10},{20,29},... | collective-permute-start | bytes 3145736 | tf_op jit(solution)/shard_map/ppermute | solution.py:477
  43.7 11.2 %collective-permute-start.6 = (f32[2,256,512]{2,1,0:T(8,128)S(1)}, f32[2,256,512]{2,1,0:T(8,128)S(1)}, u32[]{:S(2)}, u32[]{:S(2)}) collective-permute-start(f32[2,256,512]{2,1,0:T(8,128)S(1)} %get-tuple-element.38), channel_id=1, source_target_pairs={{0,2},{2,0},{5,7},{7,5},{8,10},{10,8},{13,15},{15,13},{16,18},{18,... | collective-permute-start | bytes 3145736 | tf_op jit(solution)/shard_map/ppermute | solution.py:477
  54.2 2.4 %collective-permute-start.3 = (f32[2,256,512]{2,1,0:T(8,128)S(1)}, f32[2,256,512]{2,1,0:T(8,128)S(1)}, u32[]{:S(2)}, u32[]{:S(2)}) collective-permute-start(f32[2,256,512]{2,1,0:T(8,128)S(1)} %get-tuple-element.34), channel_id=1, source_target_pairs={{0,2},{2,0},{5,7},{7,5},{8,10},{10,8},{13,15},{15,13},{16,18},{18,... | collective-permute-start | bytes 3145736 | tf_op jit(solution)/shard_map/ppermute | solution.py:477
  55.2 22.0 %collective-permute-start.7 = (f32[2,256,512]{2,1,0:T(8,128)S(1)}, f32[2,256,512]{2,1,0:T(8,128)S(1)}, u32[]{:S(2)}, u32[]{:S(2)}) collective-permute-start(f32[2,256,512]{2,1,0:T(8,128)S(1)} %add.98.full_a), channel_id=1, source_target_pairs={{0,8},{8,16},{15,7},{16,24},{23,15},{24,32},{31,23},{32,40},{39,31... | collective-permute-start | bytes 3145736 | tf_op jit(solution)/shard_map/ppermute | solution.py:477
  55.9 22.0 %collective-permute-start.9 = (f32[2,256,512]{2,1,0:T(8,128)S(1)}, f32[2,256,512]{2,1,0:T(8,128)S(1)}, u32[]{:S(2)}, u32[]{:S(2)}) collective-permute-start(f32[2,256,512]{2,1,0:T(8,128)S(1)} %add.98.full_a), channel_id=1, source_target_pairs={{0,7},{2,5},{5,2},{7,0},{8,15},{10,13},{13,10},{15,8},{16,23},{18,... | collective-permute-start | bytes 3145736 | tf_op jit(solution)/shard_map/ppermute | solution.py:477
  56.9 21.0 %collective-permute-start.8 = (f32[2,256,512]{2,1,0:T(8,128)S(1)}, f32[2,256,512]{2,1,0:T(8,128)S(1)}, u32[]{:S(2)}, u32[]{:S(2)}) collective-permute-start(f32[2,256,512]{2,1,0:T(8,128)S(1)} %add.99.full_b), channel_id=1, source_target_pairs={{0,8},{8,16},{15,7},{16,24},{23,15},{24,32},{31,23},{32,40},{39,31... | collective-permute-start | bytes 3145736 | tf_op jit(solution)/shard_map/ppermute | solution.py:477
  57.6 29.3 %collective-permute-start.4 = (f32[2,512,256]{2,1,0:T(8,128)S(1)}, f32[2,512,256]{2,1,0:T(8,128)S(1)}, u32[]{:S(2)}, u32[]{:S(2)}) collective-permute-start(f32[2,512,256]{2,1,0:T(8,128)S(1)} %get-tuple-element.35), channel_id=1, source_target_pairs={{1,2},{3,0},{4,7},{6,5},{9,10},{11,8},{12,15},{14,13},{17,18},{19,... | collective-permute-start | bytes 3145736 | tf_op jit(solution)/shard_map/ppermute | solution.py:477
  75.3 11.7 %collective-permute-start.5 = (f32[2,512,256]{2,1,0:T(8,128)S(1)}, f32[2,512,256]{2,1,0:T(8,128)S(1)}, u32[]{:S(2)}, u32[]{:S(2)}) collective-permute-start(f32[2,512,256]{2,1,0:T(8,128)S(1)} %get-tuple-element.36), channel_id=1, source_target_pairs={{1,0},{3,2},{4,5},{6,7},{9,8},{11,10},{12,13},{14,15},{17,16},{19,... | collective-permute-start | bytes 3145736 | tf_op jit(solution)/shard_map/ppermute | solution.py:477
  77.2 12.6 %collective-permute-start.10 = (f32[2,256,512]{2,1,0:T(8,128)S(1)}, f32[2,256,512]{2,1,0:T(8,128)S(1)}, u32[]{:S(2)}, u32[]{:S(2)}) collective-permute-start(f32[2,256,512]{2,1,0:T(8,128)S(1)} %add.99.full_b), channel_id=1, source_target_pairs={{0,7},{2,5},{5,2},{7,0},{8,15},{10,13},{13,10},{15,8},{16,23},{18,... | collective-permute-start | bytes 3145736 | tf_op jit(solution)/shard_map/ppermute | solution.py:477
  88.5 12.5 %collective-permute-start.12 = (f32[512,512]{1,0:T(8,128)}, f32[512,512]{1,0:T(8,128)S(1)}, u32[]{:S(2)}, u32[]{:S(2)}) collective-permute-start(f32[512,512]{1,0:T(8,128)} %get-tuple-element.46), channel_id=1, source_target_pairs={{0,1},{2,3},{5,4},{7,6},{8,9},{10,11},{13,12},{15,14},{16,17},{18,... | collective-permute-start | bytes 3145736 | tf_op jit(solution)/shard_map/ppermute | solution.py:477
  91.2 9.8 %collective-permute-start.11 = (f32[512,384]{1,0:T(8,128)}, f32[512,384]{1,0:T(8,128)}, u32[]{:S(2)}, u32[]{:S(2)}) collective-permute-start(f32[512,384]{1,0:T(8,128)} %get-tuple-element.44), channel_id=1, source_target_pairs={{0,1},{2,3},{5,4},{7,6},{8,9},{10,11},{13,12},{15,14},{16,17},{18,... | collective-permute-start | bytes 2359304 | tf_op jit(solution)/shard_map/ppermute | solution.py:477

commit v5 on v4

--- a/solution.py
+++ b/solution.py
@@ -505,7 +505,7 @@
     full_a = keep_a + came_a
     mirror_a = move(full_a, to_mirror)
     cut_a = move(full_a, to_cut)
-    send_d, keep_d, came_b = lax.optimization_barrier((send_d, keep_d, came_b))
+    send_d, came_b = lax.optimization_barrier((send_d, came_b))
     diag_in = move(send_d, to_across)
     full_b = keep_b + came_b
     cut_b = move(full_b, to_cut)

time: 104 us -> 103 us (level)
  starting transfers between devices: 38.2 us -> 36.3 us
  waiting for transfers between devices: 32.6 us -> 33.8 us
    ppermute x13, starting transfers between devices: 38.2 us -> 36.3 us  [move(): return lax.ppermute(value, AXES, route(blocks, rule))]
    ppermute x13, waiting for transfers between devices: 32.6 us -> 33.8 us  [move(): return lax.ppermute(value, AXES, route(blocks, rule))]
where the time goes in v5:
time: 103 us
  starting transfers between devices  36.3 us (35%)
  waiting for transfers between devices  33.8 us (33%)
  Pallas kernels  17.2 us (17%)
  between operations  6.69 us (6%)
  local copies, waits for them, and re-layouts  5.86 us (6%)
  other arithmetic  2.93 us (3%)
    ppermute x13, starting transfers between devices, move(): return lax.ppermute(value, AXES, route(blocks, rule))  36.3 us
    ppermute x13, waiting for transfers between devices, move(): return lax.ppermute(value, AXES, route(blocks, rule))  33.8 us
    pallas_call x1, Pallas kernels, per_device(): call(second_kernel, (rows, rows, rows, half, half, half), (vmem, vmem, vm...  6.32 us
    pallas_call x1, Pallas kernels, per_device(): call(place_kernel, wide, [vmem] * 6)  2.4 us
    pallas_call x1, Pallas kernels, per_device(): call(tiles_kernel, half, (vmem, pl.ANY), (block_of, planes))(role, own, far)  2.21 us
  transfers between devices with their start and end apart: 13, of which 4 were waited for; matrix products, arithmetic and copies ran while one was open for 7% of the time, Pallas kernels for 14%

profile of v5, /device:TPU:7, one launch (start us, length us, event | category | flops | bytes accessed | tf_op | source)
XLA Modules:
  0.0 102.7 jit_solution(2184632423702839041)
XLA Ops:
  0.0 3.5 %collective-permute-start.1 = (bf16[3,512,768]{2,1,0:T(8,128)(2,1)}, bf16[3,512,768]{2,1,0:T(8,128)(2,1)S(1)}, u32[]{:S(2)}, u32[]{:S(2)}) collective-permute-start(bf16[3,512,768]{2,1,0:T(8,128)(2,1)} %own.1), channel_id=1, source_target_pairs={{1,9},{3,11},{5,13},{7,15},{8,0},{9,17},{10,2},{11,19},{12,4},{13,... | collective-permute-start | bytes 7077896 | tf_op jit(solution)/shard_map/ppermute | solution.py:477
  3.5 3.0 %collective-permute-start = (bf16[3,512,768]{2,1,0:T(8,128)(2,1)}, bf16[3,512,768]{2,1,0:T(8,128)(2,1)}, u32[]{:S(2)}, u32[]{:S(2)}) collective-permute-start(bf16[3,512,768]{2,1,0:T(8,128)(2,1)} %own.1), channel_id=1, source_target_pairs={{0,1},{1,5},{2,3},{3,7},{4,0},{5,4},{6,2},{7,6},{8,9},{9,13},{10,1... | collective-permute-start | bytes 7077896 | tf_op jit(solution)/shard_map/ppermute | solution.py:477
  6.5 0.8 copy.6
  7.3 0.1 reduce-window.8
  7.4 0.1 reduce
  7.5 0.1 convert_reduce_fusion.1
  7.7 0.7 fusion.5
  9.7 0.7 fusion.4
  11.6 0.7 compare_reduce_fusion
  14.8 0.7 fusion.3
  16.7 0.7 fusion.1
  17.5 0.6 fusion.2
  18.1 1.3 %stack.39.role = s32[7]{0:T(128)S(1)} concatenate(s32[1]{0:T(128)} %bitcast, s32[1]{0:T(128)} %bitcast.1, s32[1]{0:T(128)} %bitcast.2, s32[1]{0:T(128)} %bitcast.8, s32[1]{0:T(128)} %bitcast.9, s32[1]{0:T(128)} %bitcast.10, s32[1]{0:T(128)} %bitcast.13), dimensions={0} | concatenate | bytes 56 | tf_op jit(solution)/shard_map/stack | solution.py:464
  19.4 0.0 copy-start
  19.4 1.7 %copy-done = bf16[3,512,768]{2,1,0:T(8,128)(2,1)S(1)} copy-done((bf16[3,512,768]{2,1,0:T(8,128)(2,1)S(1)}, bf16[3,512,768]{2,1,0:T(8,128)(2,1)}, u32[]{:S(2)}) %copy-start) | copy-done | bytes 2359320
  21.1 1.0 shard_map.28
  22.0 12.5 %collective-permute-done.1.far = bf16[3,512,768]{2,1,0:T(8,128)(2,1)S(1)} collective-permute-done((bf16[3,512,768]{2,1,0:T(8,128)(2,1)}, bf16[3,512,768]{2,1,0:T(8,128)(2,1)S(1)}, u32[]{:S(2)}, u32[]{:S(2)}) %collective-permute-start.1) | collective-permute-done | bytes 2359328 | tf_op jit(solution)/shard_map/ppermute | solution.py:477
  34.6 2.2 %shard_map.29.after = f32[2,512,256]{2,1,0:T(8,128)S(1)} custom-call(s32[7]{0:T(128)S(1)} %stack.39.role, bf16[3,512,768]{2,1,0:T(8,128)(2,1)S(1)} %get-tuple-element.25.own, bf16[3,512,768]{2,1,0:T(8,128)(2,1)S(1)} %collective-permute-done.1.far), custom_call_target="tpu_custom_call" | custom-call | tf_op jit(solution)/shard_map/pallas_call | solution.py:490
  36.8 5.2 %collective-permute-start.2 = (f32[2,512,256]{2,1,0:T(8,128)S(1)}, f32[2,512,256]{2,1,0:T(8,128)S(1)}, u32[]{:S(2)}, u32[]{:S(2)}) collective-permute-start(f32[2,512,256]{2,1,0:T(8,128)S(1)} %shard_map.29.after), channel_id=1, source_target_pairs={{4,13},{6,15},{9,0},{11,2},{12,21},{14,23},{17,8},{19,10},{20,29},... | collective-permute-start | bytes 3145736 | tf_op jit(solution)/shard_map/ppermute | solution.py:477
  42.0 0.0 collective-permute-done.mate
  42.0 1.7 %shard_map.30 = (f32[2,256,512]{2,1,0:T(8,128)S(1)}, bf16[512,768]{1,0:T(8,128)(2,1)S(1)}) custom-call(s32[7]{0:T(128)S(1)} %stack.39.role, bf16[3,512,768]{2,1,0:T(8,128)(2,1)S(1)} %get-tuple-element.25.own, bf16[512,768]{1,0:T(8,128)(2,1)S(1)} %get-tuple-element.26.own_obs, bf16[3,512,768]{2,1,0:T(8,128)(2,1)} %collective-permute-done.mate, ...), custom_call_target="tpu_custom_call" | custom-call | tf_op jit(solution)/shard_map/pallas_call | solution.py:492
  43.7 0.7 collective-permute-start.6
  44.5 6.3 %shard_map.31 = (f32[2,256,512]{2,1,0:T(8,128)S(1)}, f32[2,256,512]{2,1,0:T(8,128)S(1)}, f32[2,256,512]{2,1,0:T(8,128)S(1)}, f32[2,512,256]{2,1,0:T(8,128)S(1)},...) custom-call(s32[7]{0:T(128)S(1)} %stack.39.role, bf16[3,512,768]{2,1,0:T(8,128)(2,1)S(1)} %get-tuple-element.25.own, ...), custom_call_target="tpu_custom_call" | custom-call | tf_op jit(solution)/shard_map/pallas_call | solution.py:497
  50.8 2.9 %collective-permute-done.2.tri_in = f32[2,512,256]{2,1,0:T(8,128)S(1)} collective-permute-done((f32[2,512,256]{2,1,0:T(8,128)S(1)}, f32[2,512,256]{2,1,0:T(8,128)S(1)}, u32[]{:S(2)}, u32[]{:S(2)}) %collective-permute-start.2) | collective-permute-done | bytes 1048608 | tf_op jit(solution)/shard_map/ppermute | solution.py:477
  53.7 0.6 shard_map.32
  54.2 0.7 collective-permute-start.3
  55.0 4.0 %collective-permute-start.5 = (f32[2,512,256]{2,1,0:T(8,128)S(1)}, f32[2,512,256]{2,1,0:T(8,128)S(1)}, u32[]{:S(2)}, u32[]{:S(2)}) collective-permute-start(f32[2,512,256]{2,1,0:T(8,128)S(1)} %get-tuple-element.34), channel_id=1, source_target_pairs={{1,0},{3,2},{4,5},{6,7},{9,8},{11,10},{12,13},{14,15},{17,16},{19,... | collective-permute-start | bytes 3145736 | tf_op jit(solution)/shard_map/ppermute | solution.py:477
  59.0 0.0 collective-permute-done.6
  59.0 0.2 add.98.full_a
  59.2 0.7 collective-permute-start.7
  59.9 0.7 collective-permute-start.9
  60.7 0.0 collective-permute-done.3
  60.7 0.2 add.99.full_b
  60.9 0.7 collective-permute-start.8
  61.6 13.7 %collective-permute-start.4 = (f32[2,512,256]{2,1,0:T(8,128)S(1)}, f32[2,512,256]{2,1,0:T(8,128)S(1)}, u32[]{:S(2)}, u32[]{:S(2)}) collective-permute-start(f32[2,512,256]{2,1,0:T(8,128)S(1)} %get-tuple-element.33), channel_id=1, source_target_pairs={{1,2},{3,0},{4,7},{6,5},{9,10},{11,8},{12,15},{14,13},{17,18},{19,... | collective-permute-start | bytes 3145736 | tf_op jit(solution)/shard_map/ppermute | solution.py:477
  75.3 0.0 collective-permute-done.5.diag
  75.3 0.7 collective-permute-start.10
  76.0 0.0 collective-permute-done.7.cut_a
  76.0 0.0 collective-permute-done.9.mirror_a
  76.1 0.0 collective-permute-done.8.cut_b
  76.1 10.9 %collective-permute-done.4.diag_in = f32[2,512,256]{2,1,0:T(8,128)S(1)} collective-permute-done((f32[2,512,256]{2,1,0:T(8,128)S(1)}, f32[2,512,256]{2,1,0:T(8,128)S(1)}, u32[]{:S(2)}, u32[]{:S(2)}) %collective-permute-start.4) | collective-permute-done | bytes 1048608 | tf_op jit(solution)/shard_map/ppermute | solution.py:477
  86.9 1.5 %shard_map.33 = (f32[2,512,256]{2,1,0:T(8,128)S(1)}, f32[512,256]{1,0:T(8,128)S(1)}, f32[512,512]{1,0:T(8,128)S(1)}, f32[512,512]{1,0:T(8,128)}) custom-call(s32[7]{0:T(128)S(1)} %stack.39.role, f32[2,512,256]{2,1,0:T(8,128)S(1)} %collective-permute-done.4.diag_in, f32[2,512,256]{2,1,0:T(8,128)S(1)} %collective-permute-done.5.diag, ...), custom_call_target="tpu_custom_call" | custom-call | tf_op jit(solution)/shard_map/pallas_call | solution.py:518
  88.5 1.3 %collective-permute-start.12 = (f32[512,512]{1,0:T(8,128)}, f32[512,512]{1,0:T(8,128)S(1)}, u32[]{:S(2)}, u32[]{:S(2)}) collective-permute-start(f32[512,512]{1,0:T(8,128)} %get-tuple-element.44), channel_id=1, source_target_pairs={{0,1},{2,3},{5,4},{7,6},{8,9},{10,11},{13,12},{15,14},{16,17},{18,... | collective-permute-start | bytes 3145736 | tf_op jit(solution)/shard_map/ppermute | solution.py:477
  89.8 0.0 collective-permute-done.10.mirror_b
  89.8 1.4 %shard_map.34 = (f32[512,384]{1,0:T(8,128)}, f32[512,384]{1,0:T(8,128)S(1)}) custom-call(s32[7]{0:T(128)S(1)} %stack.39.role, f32[2,512,256]{2,1,0:T(8,128)S(1)} %get-tuple-element.39.part, f32[512,256]{1,0:T(8,128)S(1)} %get-tuple-element.40.done, f32[2,256,512]{2,1,0:T(8,128)S(1)} %collective-permute-done.10.mirror_b), custom_call_target="tpu_custom_call" | custom-call | tf_op jit(solution)/shard_map/pallas_call | solution.py:522
  91.2 1.3 %collective-permute-start.11 = (f32[512,384]{1,0:T(8,128)}, f32[512,384]{1,0:T(8,128)}, u32[]{:S(2)}, u32[]{:S(2)}) collective-permute-start(f32[512,384]{1,0:T(8,128)} %get-tuple-element.42), channel_id=1, source_target_pairs={{0,1},{2,3},{5,4},{7,6},{8,9},{10,11},{13,12},{15,14},{16,17},{18,... | collective-permute-start | bytes 2359304 | tf_op jit(solution)/shard_map/ppermute | solution.py:477
  92.5 0.1 copy.7
  92.7 0.1 convert_reduce_fusion
  92.8 7.5 %collective-permute-done.11.came = f32[512,384]{1,0:T(8,128)} collective-permute-done((f32[512,384]{1,0:T(8,128)}, f32[512,384]{1,0:T(8,128)}, u32[]{:S(2)}, u32[]{:S(2)}) %collective-permute-start.11) | collective-permute-done | bytes 786464 | tf_op jit(solution)/shard_map/ppermute | solution.py:477
  100.3 0.0 collective-permute-done.12.other
  100.3 2.4 %shard_map.35 = f32[512,640]{1,0:T(8,128)} custom-call(s32[7]{0:T(128)S(1)} %stack.39.role, s32[512,1]{1,0:T(8,128)S(1)} %fusion.row_cohort, s32[1,640]{1,0:T(1,128)S(1)} %and_select_fusion.col_cohort, f32[512,384]{1,0:T(8,128)S(1)} %get-tuple-element.41.keep, f32[512,384]{1,0:T(8,128)} %collective-permute-done.11.came, ...), custom_call_target="tpu_custom_call" | custom-call | tf_op jit(solution)/shard_map/pallas_call | solution.py:529
  (9 shorter events, 0.1 us)
Async XLA Ops:
  0.0 34.6 %collective-permute-start.1 = (bf16[3,512,768]{2,1,0:T(8,128)(2,1)}, bf16[3,512,768]{2,1,0:T(8,128)(2,1)S(1)}, u32[]{:S(2)}, u32[]{:S(2)}) collective-permute-start(bf16[3,512,768]{2,1,0:T(8,128)(2,1)} %own.1), channel_id=1, source_target_pairs={{1,9},{3,11},{5,13},{7,15},{8,0},{9,17},{10,2},{11,19},{12,4},{13,... | collective-permute-start | bytes 7077896 | tf_op jit(solution)/shard_map/ppermute | solution.py:477
  3.5 38.5 %collective-permute-start = (bf16[3,512,768]{2,1,0:T(8,128)(2,1)}, bf16[3,512,768]{2,1,0:T(8,128)(2,1)}, u32[]{:S(2)}, u32[]{:S(2)}) collective-permute-start(bf16[3,512,768]{2,1,0:T(8,128)(2,1)} %own.1), channel_id=1, source_target_pairs={{0,1},{1,5},{2,3},{3,7},{4,0},{5,4},{6,2},{7,6},{8,9},{9,13},{10,1... | collective-permute-start | bytes 7077896 | tf_op jit(solution)/shard_map/ppermute | solution.py:477
  19.4 1.7 %copy-start = (bf16[3,512,768]{2,1,0:T(8,128)(2,1)S(1)}, bf16[3,512,768]{2,1,0:T(8,128)(2,1)}, u32[]{:S(2)}) copy-start(bf16[3,512,768]{2,1,0:T(8,128)(2,1)} %own.1) | copy-start | bytes 7077892
  36.8 16.9 %collective-permute-start.2 = (f32[2,512,256]{2,1,0:T(8,128)S(1)}, f32[2,512,256]{2,1,0:T(8,128)S(1)}, u32[]{:S(2)}, u32[]{:S(2)}) collective-permute-start(f32[2,512,256]{2,1,0:T(8,128)S(1)} %shard_map.29.after), channel_id=1, source_target_pairs={{4,13},{6,15},{9,0},{11,2},{12,21},{14,23},{17,8},{19,10},{20,29},... | collective-permute-start | bytes 3145736 | tf_op jit(solution)/shard_map/ppermute | solution.py:477
  43.7 15.2 %collective-permute-start.6 = (f32[2,256,512]{2,1,0:T(8,128)S(1)}, f32[2,256,512]{2,1,0:T(8,128)S(1)}, u32[]{:S(2)}, u32[]{:S(2)}) collective-permute-start(f32[2,256,512]{2,1,0:T(8,128)S(1)} %get-tuple-element.36), channel_id=1, source_target_pairs={{0,2},{2,0},{5,7},{7,5},{8,10},{10,8},{13,15},{15,13},{16,18},{18,... | collective-permute-start | bytes 3145736 | tf_op jit(solution)/shard_map/ppermute | solution.py:477
  54.2 6.4 %collective-permute-start.3 = (f32[2,256,512]{2,1,0:T(8,128)S(1)}, f32[2,256,512]{2,1,0:T(8,128)S(1)}, u32[]{:S(2)}, u32[]{:S(2)}) collective-permute-start(f32[2,256,512]{2,1,0:T(8,128)S(1)} %get-tuple-element.32), channel_id=1, source_target_pairs={{0,2},{2,0},{5,7},{7,5},{8,10},{10,8},{13,15},{15,13},{16,18},{18,... | collective-permute-start | bytes 3145736 | tf_op jit(solution)/shard_map/ppermute | solution.py:477
  55.0 20.3 %collective-permute-start.5 = (f32[2,512,256]{2,1,0:T(8,128)S(1)}, f32[2,512,256]{2,1,0:T(8,128)S(1)}, u32[]{:S(2)}, u32[]{:S(2)}) collective-permute-start(f32[2,512,256]{2,1,0:T(8,128)S(1)} %get-tuple-element.34), channel_id=1, source_target_pairs={{1,0},{3,2},{4,5},{6,7},{9,8},{11,10},{12,13},{14,15},{17,16},{19,... | collective-permute-start | bytes 3145736 | tf_op jit(solution)/shard_map/ppermute | solution.py:477
  59.2 16.9 %collective-permute-start.7 = (f32[2,256,512]{2,1,0:T(8,128)S(1)}, f32[2,256,512]{2,1,0:T(8,128)S(1)}, u32[]{:S(2)}, u32[]{:S(2)}) collective-permute-start(f32[2,256,512]{2,1,0:T(8,128)S(1)} %add.98.full_a), channel_id=1, source_target_pairs={{0,8},{8,16},{15,7},{16,24},{23,15},{24,32},{31,23},{32,40},{39,31... | collective-permute-start | bytes 3145736 | tf_op jit(solution)/shard_map/ppermute | solution.py:477
  59.9 16.1 %collective-permute-start.9 = (f32[2,256,512]{2,1,0:T(8,128)S(1)}, f32[2,256,512]{2,1,0:T(8,128)S(1)}, u32[]{:S(2)}, u32[]{:S(2)}) collective-permute-start(f32[2,256,512]{2,1,0:T(8,128)S(1)} %add.98.full_a), channel_id=1, source_target_pairs={{0,7},{2,5},{5,2},{7,0},{8,15},{10,13},{13,10},{15,8},{16,23},{18,... | collective-permute-start | bytes 3145736 | tf_op jit(solution)/shard_map/ppermute | solution.py:477
  60.9 15.2 %collective-permute-start.8 = (f32[2,256,512]{2,1,0:T(8,128)S(1)}, f32[2,256,512]{2,1,0:T(8,128)S(1)}, u32[]{:S(2)}, u32[]{:S(2)}) collective-permute-start(f32[2,256,512]{2,1,0:T(8,128)S(1)} %add.99.full_b), channel_id=1, source_target_pairs={{0,8},{8,16},{15,7},{16,24},{23,15},{24,32},{31,23},{32,40},{39,31... | collective-permute-start | bytes 3145736 | tf_op jit(solution)/shard_map/ppermute | solution.py:477
  61.6 25.3 %collective-permute-start.4 = (f32[2,512,256]{2,1,0:T(8,128)S(1)}, f32[2,512,256]{2,1,0:T(8,128)S(1)}, u32[]{:S(2)}, u32[]{:S(2)}) collective-permute-start(f32[2,512,256]{2,1,0:T(8,128)S(1)} %get-tuple-element.33), channel_id=1, source_target_pairs={{1,2},{3,0},{4,7},{6,5},{9,10},{11,8},{12,15},{14,13},{17,18},{19,... | collective-permute-start | bytes 3145736 | tf_op jit(solution)/shard_map/ppermute | solution.py:477
  75.3 14.5 %collective-permute-start.10 = (f32[2,256,512]{2,1,0:T(8,128)S(1)}, f32[2,256,512]{2,1,0:T(8,128)S(1)}, u32[]{:S(2)}, u32[]{:S(2)}) collective-permute-start(f32[2,256,512]{2,1,0:T(8,128)S(1)} %add.99.full_b), channel_id=1, source_target_pairs={{0,7},{2,5},{5,2},{7,0},{8,15},{10,13},{13,10},{15,8},{16,23},{18,... | collective-permute-start | bytes 3145736 | tf_op jit(solution)/shard_map/ppermute | solution.py:477
  88.5 11.8 %collective-permute-start.12 = (f32[512,512]{1,0:T(8,128)}, f32[512,512]{1,0:T(8,128)S(1)}, u32[]{:S(2)}, u32[]{:S(2)}) collective-permute-start(f32[512,512]{1,0:T(8,128)} %get-tuple-element.44), channel_id=1, source_target_pairs={{0,1},{2,3},{5,4},{7,6},{8,9},{10,11},{13,12},{15,14},{16,17},{18,... | collective-permute-start | bytes 3145736 | tf_op jit(solution)/shard_map/ppermute | solution.py:477
  91.2 9.1 %collective-permute-start.11 = (f32[512,384]{1,0:T(8,128)}, f32[512,384]{1,0:T(8,128)}, u32[]{:S(2)}, u32[]{:S(2)}) collective-permute-start(f32[512,384]{1,0:T(8,128)} %get-tuple-element.42), channel_id=1, source_target_pairs={{0,1},{2,3},{5,4},{7,6},{8,9},{10,11},{13,12},{15,14},{16,17},{18,... | collective-permute-start | bytes 2359304 | tf_op jit(solution)/shard_map/ppermute | solution.py:477
